TPU v7x, 32 devices: a whole 2x2x4 slice. The times are simulated.
32 devices in a mesh: tower: 2 (over x), batch: 4 (over z), tensor: 4 (over y, core).
Axes of the slice: x: 2, y: 2, z: 4, core: 2. Of those that a mesh axis runs over, the one named last changes fastest.
Arguments:
- image_tokens: bfloat16 [9600, 768], P(('tower', 'batch', 'tensor')), may hold values from -6 to 6
- image_gains: float32 [3, 768], replicated, may hold values from 0.25 to 1.75
- image_shifts: float32 [3, 768], replicated, may hold values from -1.8 to 1.8
- image_qkv: bfloat16 [768, 3, 768], P(None, None, 'tensor'), may hold values from -0.21875 to 0.21875
- image_out: bfloat16 [768, 768], P('tensor'), may hold values from -0.875 to 0.875
- image_up: bfloat16 [768, 3072], P(None, 'tensor'), may hold values from -0.21875 to 0.21875
- image_down: bfloat16 [3072, 768], P('tensor'), may hold values from -0.21875 to 0.21875
- image_proj: bfloat16 [768, 512], replicated, may hold values from -0.21875 to 0.21875
- text_tokens: bfloat16 [14784, 512], P(('tower', 'batch', 'tensor')), may hold values from -6 to 6
- text_gains: float32 [3, 512], replicated, may hold values from 0.25 to 1.75
- text_shifts: float32 [3, 512], replicated, may hold values from -1.8 to 1.8
- text_qkv: bfloat16 [512, 3, 512], P(None, None, 'tensor'), may hold values from -0.25 to 0.25
- text_out: bfloat16 [512, 512], P('tensor'), may hold values from -1 to 1
- text_up: bfloat16 [512, 2048], P(None, 'tensor'), may hold values from -0.25 to 0.25
- text_down: bfloat16 [2048, 512], P('tensor'), may hold values from -0.25 to 0.25
- text_proj: bfloat16 [512, 512], replicated, may hold values from -0.25 to 0.25
- caption_lengths: int32 [192], P(('tower', 'batch')), may hold values from 5 to 77, as said below
- logit_scale: float32 [1], replicated, may hold values from 3.3 to 3.9
Outputs:
- image_block: bfloat16 [9600, 768], P(('tower', 'batch', 'tensor'))
- image_input_grad: bfloat16 [9600, 768], P(('tower', 'batch', 'tensor'))
- image_qkv_grad: float32 [768, 3, 768], P(None, None, 'tensor')
- image_out_grad: float32 [768, 768], P('tensor')
- image_up_grad: float32 [768, 3072], P(None, 'tensor')
- image_down_grad: float32 [3072, 768], P('tensor')
- image_gains_grad: float32 [3, 768], replicated
- image_shifts_grad: float32 [3, 768], replicated
- image_proj_grad: float32 [768, 512], replicated
- text_block: bfloat16 [14784, 512], P(('tower', 'batch', 'tensor'))
- text_input_grad: bfloat16 [14784, 512], P(('tower', 'batch', 'tensor'))
- text_qkv_grad: float32 [512, 3, 512], P(None, None, 'tensor')
- text_out_grad: float32 [512, 512], P('tensor')
- text_up_grad: float32 [512, 2048], P(None, 'tensor')
- text_down_grad: float32 [2048, 512], P('tensor')
- text_gains_grad: float32 [3, 512], replicated
- text_shifts_grad: float32 [3, 512], replicated
- text_proj_grad: float32 [512, 512], replicated
- logit_scale_grad: float32 [1], replicated
- loss: float32 [1], replicated
Inputs may be any that keep to these rules, and one draw needn't show every extreme that they name: caption_lengths[n] counts the real tokens of caption n; its end-of-text token stands at slot caption_lengths[n] - 1.
All inputs are finite; a program needn't handle non-finite values.
Results may differ from a plain program's by a relative error of at most 0.024.
Values may be sent and summed in bfloat16 or wider, within the bound.
No kernel may reach another device: no remote copies, remote signals or barrier semaphores. Data moves between devices by JAX's collectives and lax.ppermute only.
A program may use at most 192 MiB of HBM per device.

v0:
```python
import jax
import jax.numpy as jnp
from jax import lax
from jax.sharding import PartitionSpec as P

HEAD_DIM = 64
PATCHES = 50
CTX = 77


norm_eps = 1e-05
mask_fill = -1000000000.0
best_precision = lax.Precision.HIGHEST


def inner_rows(left_rows, right_rows):
    return lax.dot_general(
        left_rows, right_rows, (((0,), (0,)), ((), ())), preferred_element_type=jnp.float32
    )


def flip_dot(left_rows, right_rows):
    return lax.dot_general(
        left_rows, right_rows, (((1,), (1,)), ((), ())), preferred_element_type=jnp.float32
    )


def exact_dot(left_rows, right_rows):
    return jnp.dot(
        left_rows, right_rows, precision=best_precision, preferred_element_type=jnp.float32
    )


def exact_spread(pick_rows, values):
    return lax.dot_general(
        pick_rows,
        values,
        (((0,), (0,)), ((), ())),
        precision=best_precision,
        preferred_element_type=jnp.float32,
    )


def normalize(values, gain_row, shift_row):
    row_mean = jnp.mean(values, axis=-1, keepdims=True)
    centred = values - row_mean
    inv_dev = lax.rsqrt(jnp.mean(centred * centred, axis=-1, keepdims=True) + norm_eps)
    unit_rows = centred * inv_dev
    return (unit_rows * gain_row + shift_row, unit_rows, inv_dev)


def normalize_back(grad_rows, unit_rows, inv_dev, gain_row):
    scaled = grad_rows * gain_row
    mean_grad = jnp.mean(scaled, axis=-1, keepdims=True)
    mean_cross = jnp.mean(scaled * unit_rows, axis=-1, keepdims=True)
    grad_in = inv_dev * (scaled - mean_grad - unit_rows * mean_cross)
    return (grad_in, jnp.sum(grad_rows * unit_rows, axis=0), jnp.sum(grad_rows, axis=0))


def spread_rows(values):
    return lax.all_gather(values, "tensor", axis=0, tiled=True)


def collect_rows(left_rows, right_side, flip_right):

    def partial_term():
        if flip_right:
            return flip_dot(left_rows, right_side)
        return jnp.dot(left_rows, right_side, preferred_element_type=jnp.float32)

    return lax.psum_scatter(partial_term(), "tensor", scatter_dimension=0, tiled=True)


def split_qkv(qkv_rows, seq_count, length, head_count):
    split_heads = qkv_rows.reshape(seq_count, length, 3, head_count, HEAD_DIM)
    return (split_heads[:, :, 0], split_heads[:, :, 1], split_heads[:, :, 2])


def attend(qkv_rows, allowed, seq_count, length, head_count):
    query_part, key_part, value_part = split_qkv(qkv_rows, seq_count, length, head_count)
    scores = jnp.einsum(
        "nqhd,nkhd->nhqk", query_part, key_part, preferred_element_type=jnp.float32
    ) * HEAD_DIM ** (-0.5)
    if allowed is not None:
        scores = jnp.where(allowed[:, None], scores, mask_fill)
    row_top = jnp.max(scores, axis=-1, keepdims=True)
    weights = jnp.exp(scores - row_top)
    soft_probs = weights / jnp.sum(weights, axis=-1, keepdims=True)
    attn_mix = jnp.einsum(
        "nhqk,nkhd->nqhd",
        soft_probs.astype(jnp.bfloat16),
        value_part,
        preferred_element_type=jnp.float32,
    )
    return (
        attn_mix.astype(jnp.bfloat16).reshape(seq_count * length, head_count * HEAD_DIM),
        soft_probs,
    )


def attend_back(grad_mixed, qkv_rows, soft_probs, seq_count, length, head_count):
    query_part, key_part, value_part = split_qkv(qkv_rows, seq_count, length, head_count)
    grad_heads = grad_mixed.reshape(seq_count, length, head_count, HEAD_DIM)
    grad_value = jnp.einsum(
        "nhqk,nqhd->nkhd",
        soft_probs.astype(jnp.bfloat16),
        grad_heads,
        preferred_element_type=jnp.float32,
    )
    grad_probs = jnp.einsum(
        "nqhd,nkhd->nhqk", grad_heads, value_part, preferred_element_type=jnp.float32
    )
    grad_scores = soft_probs * (
        grad_probs - jnp.sum(soft_probs * grad_probs, axis=-1, keepdims=True)
    )
    grad_scores = grad_scores.astype(jnp.bfloat16)
    grad_query = jnp.einsum(
        "nhqk,nkhd->nqhd", grad_scores, key_part, preferred_element_type=jnp.float32
    ) * HEAD_DIM ** (-0.5)
    grad_key = jnp.einsum(
        "nhqk,nqhd->nkhd", grad_scores, query_part, preferred_element_type=jnp.float32
    ) * HEAD_DIM ** (-0.5)
    stacked = jnp.stack([grad_query, grad_key, grad_value], axis=2).astype(jnp.bfloat16)
    return stacked.reshape(seq_count * length, 3 * head_count * HEAD_DIM)


def block_forward(tokens, gain_rows, shifts, weight_set, allowed, seq_count, length):
    w_qkv, w_out, w_up, w_down = weight_set
    row_count, feature_width = tokens.shape
    head_count = w_out.shape[0] // HEAD_DIM
    residual = tokens.astype(jnp.float32)
    normed_one, unit_one, inv_one = normalize(residual, gain_rows[0], shifts[0])
    gathered_one = spread_rows(normed_one.astype(jnp.bfloat16))
    qkv_rows = jnp.dot(
        gathered_one, w_qkv.reshape(feature_width, -1), preferred_element_type=jnp.float32
    ).astype(jnp.bfloat16)
    attn_mix, soft_probs = attend(qkv_rows, allowed, seq_count, length, head_count)
    front_state = (unit_one, inv_one, gathered_one, qkv_rows, soft_probs, attn_mix)
    middle = residual + collect_rows(attn_mix, w_out, False)
    normed_two, unit_two, inv_two = normalize(middle, gain_rows[1], shifts[1])
    gathered_two = spread_rows(normed_two.astype(jnp.bfloat16))
    pre_act = jnp.dot(gathered_two, w_up, preferred_element_type=jnp.float32)
    hidden = (pre_act * jax.nn.sigmoid(1.702 * pre_act)).astype(jnp.bfloat16)
    block_final = middle + collect_rows(hidden, w_down, False)
    saved_state = front_state + (unit_two, inv_two, gathered_two, pre_act, hidden)
    return (block_final, saved_state, middle)


def attention_tail(grad_middle, grad_mixed, saved_state, gain_rows, weight_set, seq_count, length):
    w_qkv, w_out, w_up, w_down = weight_set
    unit_one, inv_one, gathered_one, qkv_rows, soft_probs = saved_state[:5]
    feature_width = w_qkv.shape[0]
    head_count = w_out.shape[0] // HEAD_DIM
    grad_qkv = attend_back(grad_mixed, qkv_rows, soft_probs, seq_count, length, head_count)
    qkv_grad = inner_rows(gathered_one, grad_qkv).reshape(w_qkv.shape)
    grad_one = collect_rows(grad_qkv, w_qkv.reshape(feature_width, -1), True)
    back_one, gain_one, shift_one = normalize_back(grad_one, unit_one, inv_one, gain_rows[0])
    grad_tokens = grad_middle + back_one
    return (grad_tokens.astype(jnp.bfloat16), qkv_grad, gain_one, shift_one)


def block_backward(grad_final, saved_state, gain_rows, weight_set, seq_count, length):
    w_qkv, w_out, w_up, w_down = weight_set
    attn_mix = saved_state[5]
    unit_two, inv_two, gathered_two, pre_act, hidden = saved_state[6:]
    grad_mlp = spread_rows(grad_final.astype(jnp.bfloat16))
    down_grad = inner_rows(hidden, grad_mlp)
    sigmoid_part = jax.nn.sigmoid(1.702 * pre_act)
    gelu_slope = sigmoid_part + 1.702 * pre_act * sigmoid_part * (1.0 - sigmoid_part)
    grad_pre = (flip_dot(grad_mlp, w_down) * gelu_slope).astype(jnp.bfloat16)
    up_grad = inner_rows(gathered_two, grad_pre)
    grad_two = collect_rows(grad_pre, w_up, True)
    back_two, gain_two, shift_two = normalize_back(grad_two, unit_two, inv_two, gain_rows[1])
    grad_middle = grad_final + back_two
    grad_branch = spread_rows(grad_middle.astype(jnp.bfloat16))
    out_grad = inner_rows(attn_mix, grad_branch)
    grad_mixed = flip_dot(grad_branch, w_out).astype(jnp.bfloat16)
    grad_tokens, qkv_grad, gain_one, shift_one = attention_tail(
        grad_middle, grad_mixed, saved_state, gain_rows, weight_set, seq_count, length
    )
    norm_grads = jnp.stack([gain_one, gain_two, shift_one, shift_two])
    return (grad_tokens, (qkv_grad, out_grad, up_grad, down_grad), norm_grads)


def head_forward(pooled, gain_rows, shifts, proj_weight):
    normed, unit_rows, inv_dev = normalize(pooled, gain_rows[2], shifts[2])
    low_normed = normed.astype(jnp.bfloat16)
    embedding = jnp.dot(low_normed, proj_weight, preferred_element_type=jnp.float32)
    inv_len = lax.rsqrt(jnp.sum(embedding * embedding, axis=-1, keepdims=True) + 1e-06)
    return (
        (embedding * inv_len).astype(jnp.bfloat16),
        (unit_rows, inv_dev, low_normed, embedding, inv_len),
    )


def head_backward(grad_unit, kept_state, gain_rows, proj_weight):
    unit_rows, inv_dev, low_normed, embedding, inv_len = kept_state
    along_norm = jnp.sum(embedding * grad_unit, axis=-1, keepdims=True)
    grad_embedding = (
        inv_len * grad_unit - inv_len * inv_len * inv_len * embedding * along_norm
    ).astype(jnp.bfloat16)
    proj_grad = inner_rows(low_normed, grad_embedding)
    grad_head = flip_dot(grad_embedding, proj_weight)
    grad_pooled, post_gain, post_shift = normalize_back(grad_head, unit_rows, inv_dev, gain_rows[2])
    return (grad_pooled, proj_grad, post_gain, post_shift)


def per_device(
    image_tokens,
    image_gains,
    image_shifts,
    image_qkv,
    image_out,
    image_up,
    image_down,
    image_proj,
    text_tokens,
    text_gains,
    text_shifts,
    text_qkv,
    text_out,
    text_up,
    text_down,
    text_proj,
    caption_lengths,
    logit_scale,
):
    pair_count = caption_lengths.shape[0]
    image_count = image_tokens.shape[0]
    text_count = text_tokens.shape[0]
    tensor_lane = lax.axis_index("tensor")
    positions = jnp.arange(CTX)
    allowed = (positions[None, None, :] <= positions[None, :, None]) & (
        positions[None, None, :] < caption_lengths[:, None, None]
    )
    image_weights = (image_qkv, image_out, image_up, image_down)
    text_weights = (text_qkv, text_out, text_up, text_down)
    image_final, image_saved, image_middle = block_forward(
        image_tokens, image_gains, image_shifts, image_weights, None, pair_count, PATCHES
    )
    text_final, text_saved, text_middle = block_forward(
        text_tokens, text_gains, text_shifts, text_weights, allowed, pair_count, CTX
    )
    image_group_spot = jnp.arange(pair_count) * PATCHES
    text_group_spot = jnp.arange(pair_count) * CTX + caption_lengths - 1
    image_spot = image_group_spot - tensor_lane * image_count
    text_spot = text_group_spot - tensor_lane * text_count
    image_pick = (jnp.arange(image_count)[None, :] == image_spot[:, None]).astype(jnp.float32)
    text_pick = (jnp.arange(text_count)[None, :] == text_spot[:, None]).astype(jnp.float32)
    image_pooled, text_pooled = lax.psum(
        (exact_dot(image_pick, image_final), exact_dot(text_pick, text_final)), "tensor"
    )
    image_unit, image_kept = head_forward(image_pooled, image_gains, image_shifts, image_proj)
    text_unit, text_kept = head_forward(text_pooled, text_gains, text_shifts, text_proj)
    image_all, text_all = (
        lax.all_gather(image_unit, ("tower", "batch"), axis=0, tiled=True),
        lax.all_gather(text_unit, ("tower", "batch"), axis=0, tiled=True),
    )
    logit_factor = jnp.exp(logit_scale[0])
    row_logits = logit_factor * flip_dot(image_unit, text_all)
    col_logits = logit_factor * flip_dot(image_all, text_unit)
    row_top = jnp.max(row_logits, axis=1, keepdims=True)
    row_lse = row_top[:, 0] + jnp.log(jnp.sum(jnp.exp(row_logits - row_top), axis=1))
    col_top = jnp.max(col_logits, axis=0, keepdims=True)
    col_lse = col_top[0] + jnp.log(jnp.sum(jnp.exp(col_logits - col_top), axis=0))
    row_all, col_all = (
        lax.all_gather(row_lse, ("tower", "batch"), axis=0, tiled=True),
        lax.all_gather(col_lse, ("tower", "batch"), axis=0, tiled=True),
    )
    pair_total = image_all.shape[0]
    own_index = lax.axis_index(("tower", "batch")) * pair_count + jnp.arange(pair_count)
    eye_rows = (jnp.arange(pair_total)[None, :] == own_index[:, None]).astype(jnp.float32)
    grad_rows = (
        0.5 * (jnp.exp(row_logits - row_lse[:, None]) + jnp.exp(row_logits - col_all[None, :]))
        - eye_rows
    )
    grad_rows = grad_rows.astype(jnp.bfloat16)
    grad_cols = (
        0.5 * (jnp.exp(col_logits - row_all[:, None]) + jnp.exp(col_logits - col_lse[None, :]))
        - eye_rows.T
    )
    grad_cols = grad_cols.astype(jnp.bfloat16)
    diag_vals = jnp.sum(row_logits * eye_rows, axis=1)
    loss_part = 0.5 * jnp.sum(row_lse - diag_vals) + 0.5 * jnp.sum(col_lse - diag_vals)
    scale_part = jnp.sum(grad_rows.astype(jnp.float32) * row_logits)
    grad_image_unit = logit_factor * jnp.dot(
        grad_rows, text_all, preferred_element_type=jnp.float32
    )
    grad_text_unit = logit_factor * inner_rows(grad_cols, image_all)
    grad_image_pooled, image_proj_grad, image_post_gain, image_post_shift = head_backward(
        grad_image_unit, image_kept, image_gains, image_proj
    )
    grad_text_pooled, text_proj_grad, text_post_gain, text_post_shift = head_backward(
        grad_text_unit, text_kept, text_gains, text_proj
    )
    text_saved = block_forward(
        text_tokens, text_gains, text_shifts, text_weights, allowed, pair_count, CTX
    )[1]
    grad_text_final = exact_spread(text_pick, grad_text_pooled)
    text_back = block_backward(
        grad_text_final, text_saved, text_gains, text_weights, pair_count, CTX
    )
    text_members = text_back[1] + (text_proj_grad, text_post_gain, text_post_shift)
    objective_members = (loss_part, scale_part)
    image_saved = block_forward(
        image_tokens, image_gains, image_shifts, image_weights, None, pair_count, PATCHES
    )[1]
    grad_image_final = exact_spread(image_pick, grad_image_pooled)
    image_back = block_backward(
        grad_image_final, image_saved, image_gains, image_weights, pair_count, PATCHES
    )
    image_members = image_back[1] + (image_proj_grad, image_post_gain, image_post_shift)
    both_sums = lax.psum(image_members + text_members + objective_members, ("tower", "batch"))
    image_sums = both_sums[:7]
    text_sums = both_sums[7:14]
    loss_sum = both_sums[14]
    scale_grad = both_sums[15]
    image_norms, text_norms = lax.psum((image_back[2], text_back[2]), ("tower", "batch", "tensor"))
    image_gains_grad = jnp.stack([image_norms[0], image_norms[1], image_sums[5]])
    image_shifts_grad = jnp.stack([image_norms[2], image_norms[3], image_sums[6]])
    text_gains_grad = jnp.stack([text_norms[0], text_norms[1], text_sums[5]])
    text_shifts_grad = jnp.stack([text_norms[2], text_norms[3], text_sums[6]])
    return (
        image_final.astype(jnp.bfloat16),
        image_back[0],
        image_sums[0],
        image_sums[1],
        image_sums[2],
        image_sums[3],
        image_gains_grad,
        image_shifts_grad,
        image_sums[4],
        text_final.astype(jnp.bfloat16),
        text_back[0],
        text_sums[0],
        text_sums[1],
        text_sums[2],
        text_sums[3],
        text_gains_grad,
        text_shifts_grad,
        text_sums[4],
        scale_grad.reshape(1),
        (loss_sum / pair_total).reshape(1),
    )


def solution(mesh):
    placed = (
        P(("tower", "batch", "tensor"), None),
        P(),
        P(),
        P(None, None, "tensor"),
        P("tensor", None),
        P(None, "tensor"),
        P("tensor", None),
        P(),
        P(("tower", "batch", "tensor"), None),
        P(),
        P(),
        P(None, None, "tensor"),
        P("tensor", None),
        P(None, "tensor"),
        P("tensor", None),
        P(),
        P(("tower", "batch")),
        P(),
    )
    return jax.shard_map(
        per_device,
        mesh=mesh,
        in_specs=placed,
        out_specs=(
            P(("tower", "batch", "tensor"), None),
            P(("tower", "batch", "tensor"), None),
            P(None, None, "tensor"),
            P("tensor", None),
            P(None, "tensor"),
            P("tensor", None),
            P(),
            P(),
            P(),
            P(("tower", "batch", "tensor"), None),
            P(("tower", "batch", "tensor"), None),
            P(None, None, "tensor"),
            P("tensor", None),
            P(None, "tensor"),
            P("tensor", None),
            P(),
            P(),
            P(),
            P(),
            P(),
        ),
        check_vma=False,
    )
```

profile of v0, /device:TPU:0, one launch (start us, length us, event | category | flops | bytes accessed | tf_op | source)
XLA Modules:
  0.0 1128.5 jit_solution(16704926193505808938)
XLA Ops:
  18.4 19.2 %all-gather.17.cloned.1.call-done = bf16[4,300,768]{2,1,0:T(8,128)(2,1)} async-done(((bf16[1,300,768]{2,1,0:T(8,128)(2,1)}), bf16[4,300,768]{2,1,0:T(8,128)(2,1)}) %all-gather.17.cloned.1.call-update) | async-done | bytes 1843216 | tf_op jit(solution)/shard_map/all_gather | solution.py:61
  39.3 3.6 convolution_convert_fusion
  42.9 6.3 reshape.321
  49.2 4.0 fusion.154
  53.2 3.5 copy.142
  56.7 3.5 copy.141
  62.6 4.1 fusion.160
  67.3 3.3 fusion.15
  73.6 3.7 fusion.172
  82.6 6.1 reshape.368
  88.7 4.2 fusion.155
  98.7 3.7 fusion.165
  108.6 68.2 %fusion.149 = (f32[304,768]{1,0:T(8,128)S(1)}, f32[464,512]{1,0:T(8,128)}) fusion(f32[1200,768]{1,0:T(8,128)} %fusion.172, f32[1848,512]{1,0:T(8,128)} %fusion.174), kind=kCustom, calls=%all-reduce-scatter.11 | all-reduce-scatter fusion | flops 1884162 | bytes 9355776
  179.5 3.5 concatenate
  186.4 3.6 collective-permute-start.2
  190.6 4.2 concatenate.2
  200.0 10.0 all-gather.19.cloned.1.call-done
  213.0 5.4 multiply_convert_fusion.2
  219.7 3.5 fusion.173
  223.2 10.3 all-gather.23.cloned.1.call-done
  236.8 5.1 multiply_convert_fusion.1
  246.2 68.3 %fusion.148 = (f32[304,768]{1,0:T(8,128)}, f32[464,512]{1,0:T(8,128)}) fusion(f32[1200,768]{1,0:T(8,128)} %fusion.173, f32[1848,512]{1,0:T(8,128)} %fusion.175), kind=kCustom, calls=%all-reduce-scatter.10 | all-reduce-scatter fusion | flops 1884162 | bytes 9355776
  324.7 4.8 concatenate.3
  331.8 11.7 %psum.141 = f32[24,512]{1,0:T(8,128)} all-reduce(f32[24,512]{1,0:T(8,128)} %fusion.79), channel_id=1, replica_groups=mesh['tower'=2,'batch'=4,'tensor'=4] {'tensor'}, use_global_device_ids=true, to_apply=%region_20.21 | all-reduce | flops 12288 | bytes 98304 | tf_op jit(solution)/shard_map/psum | solution.py:250
  349.3 4.8 concatenate.1
  356.6 33.3 %all_gather.44 = bf16[192,512]{1,0:T(8,128)(2,1)} all-gather(bf16[24,512]{1,0:T(8,128)(2,1)} %multiply_convert_fusion.5), channel_id=1, replica_groups=mesh['tower'=2,'batch'=4,'tensor'=4] {'tower','batch'}, dimensions={0}, use_global_device_ids=true | all-gather | bytes 221184 | tf_op jit(solution)/shard_map/all_gather | solution.py:257
  395.9 31.1 %all_gather.45 = bf16[192,512]{1,0:T(8,128)(2,1)S(1)} all-gather(bf16[24,512]{1,0:T(8,128)(2,1)S(1)} %multiply_convert_fusion.6), channel_id=1, replica_groups=mesh['tower'=2,'batch'=4,'tensor'=4] {'tower','batch'}, dimensions={0}, use_global_device_ids=true | all-gather | bytes 221184 | tf_op jit(solution)/shard_map/all_gather | solution.py:256
  432.5 21.9 %all-reduce.20 = (f32[192]{0:T(256)}, f32[192]{0:T(256)}) all-reduce(f32[192]{0:T(256)} %copy-done.129, f32[192]{0:T(256)} %copy-done.128), channel_id=1, replica_groups=mesh['tower'=2,'batch'=4,'tensor'=4] {'tower','batch'}, use_global_device_ids=true, to_apply=%add | all-reduce | flops 384 | bytes 3072
  475.6 5.0 all-gather.25.cloned.1.call-done
  483.3 5.2 fusion.10
  489.7 3.5 fusion.176
  493.2 11.1 all-gather.29.cloned.1.call-done
  504.4 3.3 reshape.349
  507.7 4.8 multiply_convert_fusion
  516.8 68.2 %fusion.147 = (f32[304,768]{1,0:T(8,128)S(1)}, f32[464,512]{1,0:T(8,128)}) fusion(f32[1200,768]{1,0:T(8,128)} %fusion.176, f32[1848,512]{1,0:T(8,128)} %fusion.182), kind=kCustom, calls=%all-reduce-scatter.9 | all-reduce-scatter fusion | flops 1884162 | bytes 9355776
  587.9 4.0 concatenate.4
  599.0 5.4 fusion.181
  615.5 3.5 concatenate.6
  643.4 7.5 copy.121
  650.9 6.2 convert_element_type.199
  658.7 3.9 fusion.178
  679.7 3.8 convert_element_type.211
  683.5 3.7 fusion.184
  688.6 5.2 fusion.177
  696.8 67.6 %fusion.146 = (f32[304,768]{1,0:T(8,128)S(1)}, f32[464,512]{1,0:T(8,128)S(1)}) fusion(f32[1200,768]{1,0:T(8,128)} %fusion.177, f32[1848,512]{1,0:T(8,128)} %fusion.183), kind=kCustom, calls=%all-reduce-scatter.8 | all-reduce-scatter fusion | flops 1884162 | bytes 9355776
  767.7 39.4 %all-reduce.19 = (f32[1,768]{1,0:T(1,128)}, f32[1,768]{1,0:T(1,128)}, f32[1,512]{1,0:T(1,128)}, f32[1,512]{1,0:T(1,128)}, f32[1]{0:T(128)}, /*index=5*/f32[]{:T(128)}) all-reduce(f32[1,768]{1,0:T(1,128)S(1)} %stack.91, f32[1,768]{1,0:T(1,128)S(1)} %stack.93, ...), channel_id=1, replica_groups=mesh['tower'=2,'batch'=4,'tensor'=4] {'tower','batch'}, use_global_device_ids=true, to_apply=%region_48.49 | all-reduce | flops 2562 | bytes 20496 | tf_op jit(solution)/shard_map/psum | solution.py:313
  817.2 42.3 %all-reduce.18 = (f32[4,768]{1,0:T(4,128)S(1)}, f32[4,512]{1,0:T(4,128)S(1)}) all-reduce(f32[4,768]{1,0:T(4,128)S(1)} %pad_maximum_fusion, f32[4,512]{1,0:T(4,128)S(1)} %pad_maximum_fusion.3), channel_id=1, replica_groups=mesh['tower'=2,'batch'=4,'tensor'=4] {'tower','batch','tensor'}, use_global_device_ids=true, to_apply=%region_46.47 | all-reduce | flops 5120 | bytes 40960 | tf_op jit(solution)/shard_map/psum | solution.py:318
  863.2 242.4 %all-reduce.31.cloned.1.call-done = (f32[768,3,192]{0,2,1:T(8,128)}, f32[192,768]{1,0:T(8,128)}, f32[768,768]{1,0:T(8,128)}, f32[768,768]{1,0:T(8,128)}, f32[768...) async-done(((f32[768,3,192]{0,2,1:T(8,128)}, f32[192,768]{1,0:T(8,128)}, ...) | async-done | bytes 12845072 | tf_op jit(solution)/shard_map/psum | solution.py:313
  (487 shorter events, 215.9 us)
Async XLA Ops:
  7.2 205.8 %copy-start = (bf16[768,768]{1,0:T(8,128)(2,1)S(1)}, bf16[768,768]{1,0:T(8,128)(2,1)}, u32[]{:S(2)}) copy-start(bf16[768,768]{1,0:T(8,128)(2,1)} %param.23) | copy-start | bytes 3538948
  7.2 30.4 %all-gather.17.cloned.1.call-start = ((), (), s32[]{:S(2)}) async-start(), calls=%async_computation.1 | async-start | bytes 2334720 | tf_op jit(solution)/shard_map/all_gather | solution.py:61
  13.5 63.8 %all-gather.21.cloned.1.call-start = ((), (), s32[]{:S(2)}) async-start(), calls=%async_computation.3 | async-start | bytes 2375680 | tf_op jit(solution)/shard_map/all_gather | solution.py:61
  16.3 193.7 %all-gather.19.cloned.1.call-start = ((), (), s32[]{:S(2)}) async-start(), calls=%async_computation.2 | async-start | bytes 2334720 | tf_op jit(solution)/shard_map/all_gather | solution.py:61
  108.6 69.6 %copy-start.131 = (u32[32]{0:T(128)S(1)}, u32[32]{0:T(128)}, u32[]{:S(2)}) copy-start(u32[32]{0:T(128)} %constant.105) | copy-start | bytes 388
  176.8 2.7 collective-permute-start
  184.7 11.6 %copy-start.89 = (f32[300]{0:T(512)}, f32[300]{0:T(512)S(1)}, u32[]{:S(2)}) copy-start(f32[300]{0:T(512)S(1)} %add_rsqrt_fusion.2) | copy-start | bytes 3604
  185.7 47.8 %all-gather.23.cloned.1.call-start = ((), (), s32[]{:S(2)}) async-start(), calls=%async_computation.4 | async-start | bytes 2375680 | tf_op jit(solution)/shard_map/all_gather | solution.py:61
  186.4 4.2 collective-permute-start.2
  196.3 16.6 %copy-start.73 = (f32[462]{0:T(512)}, f32[462]{0:T(512)S(1)}, u32[]{:S(2)}) copy-start(f32[462]{0:T(512)S(1)} %broadcast_multiply_fusion.4) | copy-start | bytes 5548
  198.2 191.7 %all-reduce.29.cloned.1.call-start = ((), (), s32[]{:S(2)}) async-start(), calls=%async_computation | async-start | bytes 147456 | tf_op jit(solution)/shard_map/psum | solution.py:250
  246.2 72.7 %copy-start.133 = (u32[32]{0:T(128)S(1)}, u32[32]{0:T(128)}, u32[]{:S(2)}) copy-start(u32[32]{0:T(128)} %constant.93) | copy-start | bytes 388
  315.8 8.9 collective-permute-start.3
  321.6 25.0 %copy-start.75 = (f32[1,512]{1,0:T(1,128)S(1)}, f32[1,512]{1,0:T(1,128)}, u32[]{:S(2)}) copy-start(f32[1,512]{1,0:T(1,128)} %get-tuple-element.114) | copy-start | bytes 6148
  321.6 27.8 %collective-permute-start.1 = (f32[12,768]{1,0:T(8,128)}, f32[12,768]{1,0:T(8,128)}, u32[]{:S(2)}, u32[]{:S(2)}) collective-permute-start(f32[12,768]{1,0:T(8,128)} %slice.133), channel_id=1, source_target_pairs={{0,1},{1,2},{2,3},{4,5},{5,6},{6,7},{8,9},{9,10},{10,11},{12,13},{... | collective-permute-start | bytes 110600
  356.5 124.1 %all-gather.25.cloned.1.call-start = ((), (), s32[]{:S(2)}) async-start(), calls=%async_computation.5 | async-start | bytes 2334720 | tf_op jit(solution)/shard_map/all_gather | solution.py:61
  392.1 38.6 %copy-start.103 = (f32[24]{0:T(128)}, f32[24]{0:T(128)S(1)}, u32[]{:S(2)}) copy-start(f32[24]{0:T(128)S(1)} %broadcast_multiply_fusion.17) | copy-start | bytes 292
  393.2 37.6 %copy-start.109 = (f32[24]{0:T(128)}, f32[24]{0:T(128)S(1)}, u32[]{:S(2)}) copy-start(f32[24]{0:T(128)S(1)} %add_rsqrt_fusion.7) | copy-start | bytes 292
  394.8 33.9 %copy-start.52 = (f32[24,512]{1,0:T(8,128)}, f32[24,512]{1,0:T(8,128)S(1)}, u32[]{:S(2)}) copy-start(f32[24,512]{1,0:T(8,128)S(1)} %get-tuple-element.135) | copy-start | bytes 147460
  462.0 42.4 %all-gather.29.cloned.1.call-start = ((), (), s32[]{:S(2)}) async-start(), calls=%async_computation.7 | async-start | bytes 2375680 | tf_op jit(solution)/shard_map/all_gather | solution.py:61
  469.5 155.3 %all-gather.27.cloned.1.call-start = ((), (), s32[]{:S(2)}) async-start(), calls=%async_computation.6 | async-start | bytes 2334720 | tf_op jit(solution)/shard_map/all_gather | solution.py:61
  493.2 14.4 %copy-start.55 = (bf16[512,512]{1,0:T(8,128)(2,1)S(1)}, bf16[512,512]{1,0:T(8,128)(2,1)}, u32[]{:S(2)}) copy-start(bf16[512,512]{1,0:T(8,128)(2,1)} %param.32) | copy-start | bytes 1572868
  516.7 69.5 %copy-start.31 = (f32[24,768]{1,0:T(8,128)S(1)}, f32[24,768]{1,0:T(8,128)}, u32[]{:S(2)}) copy-start(f32[24,768]{1,0:T(8,128)} %all-reduce.29.cloned.1.call-done) | copy-start | bytes 221188
  516.7 69.5 %copy-start.68 = (bf16[24,512]{1,0:T(8,128)(2,1)S(1)}, bf16[24,512]{1,0:T(8,128)(2,1)}, u32[]{:S(2)}) copy-start(bf16[24,512]{1,0:T(8,128)(2,1)} %copy-done.67) | copy-start | bytes 73732
  516.7 69.6 %copy-start.80 = (f32[768]{0:T(1024)S(1)}, f32[768]{0:T(1024)}, u32[]{:S(2)}) copy-start(f32[768]{0:T(1024)} %get-tuple-element.49) | copy-start | bytes 9220
  516.7 69.6 %copy-start.104 = (f32[24]{0:T(128)S(1)}, f32[24]{0:T(128)}, u32[]{:S(2)}) copy-start(f32[24]{0:T(128)} %copy-done.103) | copy-start | bytes 292
  516.8 69.6 %copy-start.110 = (f32[24]{0:T(128)S(1)}, f32[24]{0:T(128)}, u32[]{:S(2)}) copy-start(f32[24]{0:T(128)} %copy-done.109) | copy-start | bytes 292
  585.0 3.0 collective-permute-start.4
  597.3 65.3 %all-gather.31.cloned.1.call-start = ((), (), s32[]{:S(2)}) async-start(), calls=%async_computation.8 | async-start | bytes 2375680 | tf_op jit(solution)/shard_map/all_gather | solution.py:61
  607.7 7.8 collective-permute-start.6
  624.4 481.2 %all-reduce.31.cloned.1.call-start = ((), (), s32[]{:S(2)}) async-start(), calls=%async_computation.9 | async-start | bytes 25690112 | tf_op jit(solution)/shard_map/psum | solution.py:313
  696.8 69.0 %copy-start.118 = (f32[24]{0:T(128)S(1)}, f32[24]{0:T(128)}, u32[]{:S(2)}) copy-start(f32[24]{0:T(128)} %get-tuple-element.97) | copy-start | bytes 292
  696.8 69.6 %copy-start.97 = (f32[768]{0:T(1024)S(1)}, f32[768]{0:T(1024)}, u32[]{:S(2)}) copy-start(f32[768]{0:T(1024)} %get-tuple-element.36) | copy-start | bytes 9220
  696.8 69.6 %copy-start.96 = (f32[768]{0:T(1024)S(1)}, f32[768]{0:T(1024)}, u32[]{:S(2)}) copy-start(f32[768]{0:T(1024)} %get-tuple-element.41) | copy-start | bytes 9220
  696.8 70.9 %copy-start.112 = (f32[512]{0:T(512)S(1)}, f32[512]{0:T(512)}, u32[]{:S(2)}) copy-start(f32[512]{0:T(512)} %get-tuple-element.38) | copy-start | bytes 6148
  696.8 70.9 %copy-start.113 = (f32[512]{0:T(512)S(1)}, f32[512]{0:T(512)}, u32[]{:S(2)}) copy-start(f32[512]{0:T(512)} %get-tuple-element.43) | copy-start | bytes 6148
  696.8 111.0 %copy-start.100 = (f32[768]{0:T(1024)S(1)}, f32[768]{0:T(1024)}, u32[]{:S(2)}) copy-start(f32[768]{0:T(1024)} %get-tuple-element.22) | copy-start | bytes 9220
  696.8 111.6 %copy-start.99 = (f32[768]{0:T(1024)S(1)}, f32[768]{0:T(1024)}, u32[]{:S(2)}) copy-start(f32[768]{0:T(1024)} %get-tuple-element.31) | copy-start | bytes 9220
  764.4 47.7 %copy-start.72 = (f32[462]{0:T(512)S(1)}, f32[462]{0:T(512)}, u32[]{:S(2)}) copy-start(f32[462]{0:T(512)} %copy-done.71) | copy-start | bytes 5548
  764.5 47.7 %copy-start.82 = (f32[462]{0:T(512)S(1)}, f32[462]{0:T(512)}, u32[]{:S(2)}) copy-start(f32[462]{0:T(512)} %copy-done.81) | copy-start | bytes 5548
  764.5 47.7 %copy-start.84 = (f32[1,512]{1,0:T(1,128)S(1)}, f32[1,512]{1,0:T(1,128)}, u32[]{:S(2)}) copy-start(f32[1,512]{1,0:T(1,128)} %copy-done.83) | copy-start | bytes 6148
  764.5 46.4 %collective-permute-start.7 = (f32[6,512]{1,0:T(8,128)S(1)}, f32[6,512]{1,0:T(8,128)S(1)}, u32[]{:S(2)}, u32[]{:S(2)}) collective-permute-start(f32[6,512]{1,0:T(8,128)S(1)} %slice.139), channel_id=1, source_target_pairs={{0,1},{1,2},{2,3},{4,5},{5,6},{6,7},{8,9},{9,10},{10,11},{12,13},{... | collective-permute-start | bytes 36872
  809.0 5.7 collective-permute-start.5
  814.6 44.9 %copy-start.127 = (f32[1,512]{1,0:T(1,128)S(1)}, f32[1,512]{1,0:T(1,128)}, u32[]{:S(2)}) copy-start(f32[1,512]{1,0:T(1,128)} %get-tuple-element.59) | copy-start | bytes 6148
  814.6 45.5 %copy-start.126 = (f32[1,512]{1,0:T(1,128)S(1)}, f32[1,512]{1,0:T(1,128)}, u32[]{:S(2)}) copy-start(f32[1,512]{1,0:T(1,128)} %get-tuple-element.58) | copy-start | bytes 6148
  814.6 46.1 %copy-start.123 = (f32[1,768]{1,0:T(1,128)S(1)}, f32[1,768]{1,0:T(1,128)}, u32[]{:S(2)}) copy-start(f32[1,768]{1,0:T(1,128)} %get-tuple-element.57) | copy-start | bytes 9220
  814.7 46.8 %copy-start.122 = (f32[1,768]{1,0:T(1,128)S(1)}, f32[1,768]{1,0:T(1,128)}, u32[]{:S(2)}) copy-start(f32[1,768]{1,0:T(1,128)} %get-tuple-element.56) | copy-start | bytes 9220
  814.7 47.4 %copy-start.27 = (f32[300,768]{1,0:T(8,128)S(1)}, f32[300,768]{1,0:T(8,128)}, u32[]{:S(2)}) copy-start(f32[300,768]{1,0:T(8,128)} %get-tuple-element.93) | copy-start | bytes 2764804
  (107 other events, 326.1 us)
Sparse Core Ops, SparseCore 0:
  13.6 23.9 all-gather.16
  39.8 21.4 all-gather.20
  185.8 24.1 all-gather.18
  212.0 21.4 all-gather.22
  356.6 29.8 all-reduce.28
  462.1 18.4 all-gather.24
  482.8 21.5 all-gather.28
  597.5 23.7 all-gather.26
  624.5 23.1 all-gather.30
  687.4 418.1 all-reduce.30
where the time goes:
time: 1140 us; the launch traced here: 1130 us
  blocking collectives  452 us (40%)
  waiting for transfers between devices  298 us (26%)
  local copies, waits for them, and re-layouts  161 us (14%)
  matrix products  126 us (11%)
  other arithmetic  50.5 us (4%)
  between operations  21.7 us (2%)
  starting transfers between devices  18.7 us (2%)
    unnamed x5, blocking collectives  294 us
    psum x1, waiting for transfers between devices, per_device(): lax.psum(image_members + text_members + objective_members, ('tower', 'bat...  242 us
    unnamed x321, local copies, waits for them, and re-layouts  104 us
    all_gather x8, waiting for transfers between devices, spread_rows(): return lax.all_gather(values, 'tensor', axis=0, tiled=True)  55.6 us
    psum x1, blocking collectives, per_device(): lax.psum((image_back[2], text_back[2]), ('tower', 'batch', 'tensor'))  42.3 us
    psum x1, blocking collectives, per_device(): lax.psum(image_members + text_members + objective_members, ('tower', 'bat...  39.4 us
    dot_general x12, matrix products, flip_dot(): lax.dot_general(left_rows, right_rows, (((1,), (1,)), ((), ())), preferre...  33.9 us
    all_gather x1, blocking collectives, per_device(): lax.all_gather(text_unit, ('tower', 'batch'), axis=0, tiled=True)  33.3 us
  transfers between devices with their start and end apart: 18, of which 6 were waited for; matrix products, arithmetic and copies ran while one was open for 22% of the time, Pallas kernels for 0%

commit v1 on v0

v1 whole, which is shorter than its diff:
```python
import jax
import jax.numpy as jnp
from jax import lax
from jax.sharding import Mesh, PartitionSpec as P

HEAD = 64
PATCHES = 50
CTX = 77
EPS = 1e-05
F32 = jnp.float32
BF16 = jnp.bfloat16
HIGH = lax.Precision.HIGHEST
SCALE = HEAD**-0.5
SWAP = [(0, 1), (1, 0)]


def nn(a, b):
    return lax.dot_general(a, b, (((1,), (0,)), ((), ())), preferred_element_type=F32)


def nt(a, b):
    return lax.dot_general(a, b, (((1,), (1,)), ((), ())), preferred_element_type=F32)


def tn(a, b):
    return lax.dot_general(a, b, (((0,), (0,)), ((), ())), preferred_element_type=F32)


def exact_nn(a, b):
    return lax.dot_general(
        a, b, (((1,), (0,)), ((), ())), precision=HIGH, preferred_element_type=F32
    )


def exact_tn(a, b):
    return lax.dot_general(
        a, b, (((0,), (0,)), ((), ())), precision=HIGH, preferred_element_type=F32
    )


def iota(shape, dim):
    return lax.broadcasted_iota(jnp.int32, shape, dim)


def norm_parts(v):
    mean = jnp.mean(v, axis=-1, keepdims=True)
    centred = v - mean
    inv = lax.rsqrt(jnp.mean(centred * centred, axis=-1, keepdims=True) + EPS)
    return centred * inv, inv


def norm_back(o, unit, inv, gain):
    scaled = o * gain
    mean_o = jnp.mean(scaled, axis=-1, keepdims=True)
    mean_u = jnp.mean(scaled * unit, axis=-1, keepdims=True)
    back = inv * (scaled - mean_o - unit * mean_u)
    return back, jnp.sum(o * unit, axis=0, keepdims=True), jnp.sum(o, axis=0, keepdims=True)


def sigmoid(v):
    return 1.0 / (1.0 + jnp.exp(-v))


def into(a, w, flip):
    return nt(a, w) if flip else nn(a, w)


def outof(a, w, flip):
    return nn(a, w) if flip else nt(a, w)


def head_mask(heads):
    shape = (heads * 8, heads * HEAD)
    return iota(shape, 0) // 8 == iota(shape, 1) // HEAD


def seq_mask(lens, heads, length, rows):
    lens_all = jnp.concatenate([lens] * heads, axis=0)
    shape = (heads * 8, rows)
    low = (iota(shape, 0) % 8) * length
    col = iota(shape, 1)
    return (col >= low) & (col < low + lens_all)


def pick_rows(lens, length, rows):
    shape = (8, rows)
    back = lens - 1 if length == CTX else 0
    spot = jnp.where(lens > 0, iota((8, 1), 0) * length + back, -1)
    return iota(shape, 1) == spot


def spread_heads(rows, mask, heads):
    return jnp.where(mask, jnp.concatenate([rows.astype(F32)] * heads, axis=0), 0.0)


def fold_heads(rows, mask, heads):
    kept = jnp.where(mask, rows, 0.0)
    total = kept[:8]
    for h in range(1, heads):
        total = total + kept[8 * h : 8 * h + 8]
    return total


def pooled_front(cfg, tokens, gains, shifts, lens, wq, wk, wv, wo):
    length, heads, flip = cfg
    rows = tokens.shape[0]
    unit, _ = norm_parts(tokens.astype(F32))
    normed = (unit * gains[0:1] + shifts[0:1]).astype(BF16)
    pick = pick_rows(lens, length, rows).astype(BF16)
    middle = nn(pick, tokens)
    normed_pick = nn(pick, normed).astype(BF16)
    allowed = seq_mask(lens, heads, length, rows)
    mask = head_mask(heads)
    keys, values, probs, queries, mixes, y_vals = [], [], [], [], [], []
    for s in range(4):
        key = into(normed, wk[s], flip).astype(BF16)
        value = into(normed, wv[s], flip).astype(BF16)
        query = into(normed_pick, wq[s], flip).astype(BF16)
        scores = nt(spread_heads(query, mask, heads).astype(BF16), key) * SCALE
        scores = jnp.where(allowed, scores, -1e9)
        weights = jnp.where(allowed, jnp.exp(scores - jnp.max(scores, axis=-1, keepdims=True)), 0.0)
        total = jnp.sum(weights, axis=-1, keepdims=True)
        prob = weights / jnp.where(total > 0.0, total, 1.0)
        low = prob.astype(BF16)
        mix = fold_heads(nn(low, value), mask, heads).astype(BF16)
        middle = middle + nn(mix, wo[s])
        y_vals.append(nn(low, normed).astype(BF16))
        keys.append(key)
        values.append(value)
        probs.append(prob)
        queries.append(query)
        mixes.append(mix)
    return middle, normed, normed_pick, keys, values, probs, queries, mixes, y_vals


def bulk(cfg, tokens, gains, shifts, lens, normed, keys, values, wq, wo, up, down):
    length, heads, flip = cfg
    rows = tokens.shape[0]
    seqs = rows // length
    middle = tokens.astype(F32)
    pos = jnp.arange(length)
    allowed = pos[None, None, :] < lens[:seqs, 0][:, None, None]
    if length == CTX:
        allowed = allowed & (pos[None, None, :] <= pos[None, :, None])
    for s in range(4):
        query = into(normed, wq[s], flip).astype(BF16).reshape(seqs, length, heads, HEAD)
        key = keys[s].reshape(seqs, length, heads, HEAD)
        value = values[s].reshape(seqs, length, heads, HEAD)
        scores = jnp.einsum("nqhd,nkhd->nhqk", query, key, preferred_element_type=F32) * SCALE
        scores = jnp.where(allowed[:, None], scores, -1e9)
        weights = jnp.exp(scores - jnp.max(scores, axis=-1, keepdims=True))
        prob = (weights / jnp.sum(weights, axis=-1, keepdims=True)).astype(BF16)
        mix = jnp.einsum("nhqk,nkhd->nqhd", prob, value, preferred_element_type=F32)
        middle = middle + nn(mix.astype(BF16).reshape(rows, heads * HEAD), wo[s])
    unit, _ = norm_parts(middle)
    normed_two = (unit * gains[1:2] + shifts[1:2]).astype(BF16)
    final = middle
    for s in range(4):
        pre = nn(normed_two, up[s])
        final = final + nn((pre * sigmoid(1.702 * pre)).astype(BF16), down[s])
    return final.astype(BF16)


def mlp_head_forward(middle, gains, shifts, up, down, proj):
    unit_two, inv_two = norm_parts(middle)
    normed_two = (unit_two * gains[1:2] + shifts[1:2]).astype(BF16)
    final = middle
    pres, hids = [], []
    for s in range(4):
        pre = nn(normed_two, up[s])
        hid = (pre * sigmoid(1.702 * pre)).astype(BF16)
        final = final + nn(hid, down[s])
        pres.append(pre)
        hids.append(hid)
    unit_head, inv_head = norm_parts(final)
    normed_head = (unit_head * gains[2:3] + shifts[2:3]).astype(BF16)
    embedding = nn(normed_head, proj)
    inv_len = lax.rsqrt(jnp.sum(embedding * embedding, axis=-1, keepdims=True) + 1e-06)
    unit = (embedding * inv_len).astype(BF16)
    return unit, (unit_two, inv_two, normed_two, pres, hids, unit_head, inv_head, normed_head, embedding, inv_len)


def mlp_head_backward(grad_unit, kept, gains, up, down, proj, wo_own, mix_own):
    unit_two, inv_two, normed_two, pres, hids, unit_head, inv_head, normed_head, embedding, inv_len = kept
    along = jnp.sum(embedding * grad_unit, axis=-1, keepdims=True)
    grad_emb = (inv_len * grad_unit - inv_len * inv_len * inv_len * embedding * along).astype(BF16)
    proj_grad = tn(normed_head, grad_emb)
    grad_final, gain_2, shift_2 = norm_back(nt(grad_emb, proj), unit_head, inv_head, gains[2:3])
    grad_mlp = grad_final.astype(BF16)
    grad_two = None
    for s in range(4):
        gate = sigmoid(1.702 * pres[s])
        slope = gate + 1.702 * pres[s] * gate * (1.0 - gate)
        grad_pre = (nt(grad_mlp, down[s]) * slope).astype(BF16)
        part = nt(grad_pre, up[s])
        grad_two = part if grad_two is None else grad_two + part
        if s == 0:
            down_grad = tn(hids[0], grad_mlp)
            up_grad = tn(normed_two, grad_pre)
    back, gain_1, shift_1 = norm_back(grad_two, unit_two, inv_two, gains[1:2])
    grad_middle = grad_final + back
    branch = grad_middle.astype(BF16)
    out_grad = tn(mix_own, branch)
    mixed_own = nt(branch, wo_own).astype(BF16)
    return grad_middle, mixed_own, out_grad, up_grad, down_grad, proj_grad, (gain_1, gain_2), (shift_1, shift_2)


def contrast(image_unit, text_unit, logit_scale):
    factor = jnp.exp(logit_scale)
    logits = factor * nt(image_unit, text_unit)
    count = logits.shape[0]
    row_top = jnp.max(logits, axis=1, keepdims=True)
    row_lse = row_top + jnp.log(jnp.sum(jnp.exp(logits - row_top), axis=1, keepdims=True))
    col_top = jnp.max(logits, axis=0, keepdims=True)
    col_lse = col_top + jnp.log(jnp.sum(jnp.exp(logits - col_top), axis=0, keepdims=True))
    eye = iota(logits.shape, 0) == iota(logits.shape, 1)
    diag = jnp.sum(jnp.where(eye, logits, 0.0))
    loss = (0.5 * (jnp.sum(row_lse) + jnp.sum(col_lse)) - diag) / count
    grad = 0.5 * (jnp.exp(logits - row_lse) + jnp.exp(logits - col_lse))
    grad = jnp.where(eye, grad - 1.0, grad).astype(BF16)
    scale_grad = jnp.sum(grad.astype(F32) * logits)
    grad_image = factor * nn(grad, text_unit)
    grad_text = factor * tn(grad, image_unit)
    return loss, scale_grad, grad_image, grad_text


def attention_back(cfg, tokens, gains, shifts, lens, grad_rows, normed, keys, values, probs, queries, wq, wk, wv, wo):
    length, heads, flip = cfg
    rows = tokens.shape[0]
    unit, inv = norm_parts(tokens.astype(F32))
    mask = head_mask(heads)
    branch = grad_rows.astype(BF16)
    left, right, y_keys, g_queries = [], [], [], []
    query_side = None
    for s in range(4):
        grad_mixed = nt(branch, wo[s]).astype(BF16)
        spread = spread_heads(grad_mixed, mask, heads).astype(BF16)
        grad_probs = nt(spread, values[s])
        prob = probs[s]
        grad_scores = (prob * (grad_probs - jnp.sum(prob * grad_probs, axis=-1, keepdims=True))).astype(BF16)
        grad_query = (fold_heads(nn(grad_scores, keys[s]), mask, heads) * SCALE).astype(BF16)
        part = outof(grad_query, wq[s], flip)
        query_side = part if query_side is None else query_side + part
        wide = (spread_heads(queries[s], mask, heads) * SCALE).astype(BF16)
        left += [grad_scores, prob.astype(BF16)]
        right += [outof(wide, wk[s], flip).astype(BF16), outof(spread, wv[s], flip).astype(BF16)]
        y_keys.append(nn(grad_scores, normed).astype(BF16))
        g_queries.append(grad_query)
    pick = pick_rows(lens, length, rows)
    grad_one = tn(jnp.concatenate(left, axis=0), jnp.concatenate(right, axis=0))
    grad_one = grad_one + tn(pick.astype(BF16), query_side.astype(BF16))
    back, gain_0, shift_0 = norm_back(grad_one, unit, inv, gains[0:1])
    grad_tokens = exact_tn(pick.astype(F32), grad_rows) + back
    return grad_tokens.astype(BF16), gain_0, shift_0, y_keys, g_queries


def per_device(
    image_tokens, image_gains, image_shifts, image_qkv, image_out, image_up, image_down, image_proj,
    text_tokens, text_gains, text_shifts, text_qkv, text_out, text_up, text_down, text_proj,
    caption_lengths, logit_scale,
):
    every = ("x", "zh", "zb", "y", "c")
    devices = lax.axis_size(every)
    groups = devices // 4
    lane = lax.axis_index(("y", "c"))
    seqs = image_tokens.shape[0] // PATCHES
    image_cfg = (PATCHES, image_out.shape[0] // HEAD, True)
    text_cfg = (CTX, text_out.shape[0] // HEAD, False)
    image_lens = jnp.where(iota((8, 1), 0) < seqs, PATCHES, 0)
    own_lens = lax.dynamic_slice(caption_lengths, (lane * seqs,), (seqs,))
    text_lens = jnp.pad(own_lens, (0, 8 - seqs)).reshape(8, 1)

    def gather(w):
        over_y = lax.ppermute(w, "y", SWAP)
        return [w, over_y, lax.ppermute(w, "c", SWAP), lax.ppermute(over_y, "c", SWAP)]

    image_w = gather(jnp.transpose(image_qkv, (1, 2, 0)))
    text_w = gather(jnp.transpose(text_qkv, (1, 0, 2)))
    image_q, image_k, image_v = ([w[i] for w in image_w] for i in range(3))
    text_q, text_k, text_v = ([w[i] for w in text_w] for i in range(3))
    image_o, text_o = gather(image_out), gather(text_out)
    image_u, image_d = gather(image_up), gather(image_down)
    text_u, text_d = gather(text_up), gather(text_down)

    im = pooled_front(image_cfg, image_tokens, image_gains, image_shifts, image_lens, image_q, image_k, image_v, image_o)
    tx = pooled_front(text_cfg, text_tokens, text_gains, text_shifts, text_lens, text_q, text_k, text_v, text_o)

    def everywhere(v):
        wide = jnp.broadcast_to(v[None], (devices,) + v.shape)
        return lax.all_to_all(wide, every, split_axis=0, concat_axis=0, tiled=True)

    def to_lanes(slots):
        order = jnp.arange(4) ^ lane
        slot_of = order // 2 % 2 + order % 2 * 2
        v = jnp.take(jnp.stack(slots), slot_of, axis=0)
        wide = jnp.broadcast_to(v[None], (groups,) + v.shape).reshape((devices,) + v.shape[1:])
        return lax.all_to_all(wide, every, split_axis=0, concat_axis=0, tiled=True)

    def compact(v):
        return v[:, :seqs].reshape(devices * seqs, v.shape[-1])

    width = image_tokens.shape[1]
    mids = everywhere(jnp.concatenate([im[0], tx[0]], axis=1))
    image_mid, text_mid = compact(mids[:, :, :width]), compact(mids[:, :, width:])
    image_mix, text_mix = compact(to_lanes(im[7])), compact(to_lanes(tx[7]))
    image_first, text_first = compact(everywhere(im[2])), compact(everywhere(tx[2]))

    def by_head(y, heads):
        y = y.reshape(devices, heads, 8, y.shape[-1])[:, :, :seqs]
        return jnp.swapaxes(y, 0, 1).reshape(heads, devices * seqs, y.shape[-1])

    image_yv, text_yv = by_head(to_lanes(im[8]), image_cfg[1]), by_head(to_lanes(tx[8]), text_cfg[1])

    image_block = bulk(image_cfg, image_tokens, image_gains, image_shifts, image_lens, im[1], im[3], im[4], image_q, image_o, image_u, image_d)
    text_block = bulk(text_cfg, text_tokens, text_gains, text_shifts, text_lens, tx[1], tx[3], tx[4], text_q, text_o, text_u, text_d)

    image_unit, image_kept = mlp_head_forward(image_mid, image_gains, image_shifts, image_u, image_d, image_proj)
    text_unit, text_kept = mlp_head_forward(text_mid, text_gains, text_shifts, text_u, text_d, text_proj)
    loss, scale_grad, grad_image, grad_text = contrast(image_unit, text_unit, logit_scale[0])
    ib = mlp_head_backward(grad_image, image_kept, image_gains, image_u, image_d, image_proj, image_out, image_mix)
    tb = mlp_head_backward(grad_text, text_kept, text_gains, text_u, text_d, text_proj, text_out, text_mix)

    me = lax.axis_index(every)

    def own_rows(v):
        return jnp.pad(lax.dynamic_slice(v, (me * seqs, 0), (seqs, v.shape[1])), ((0, 8 - seqs), (0, 0)))

    ia = attention_back(image_cfg, image_tokens, image_gains, image_shifts, image_lens, own_rows(ib[0]), im[1], im[3], im[4], im[5], im[6], image_q, image_k, image_v, image_o)
    ta = attention_back(text_cfg, text_tokens, text_gains, text_shifts, text_lens, own_rows(tb[0]), tx[1], tx[3], tx[4], tx[5], tx[6], text_q, text_k, text_v, text_o)
    image_yk, text_yk = by_head(to_lanes(ia[3]), image_cfg[1]), by_head(to_lanes(ta[3]), text_cfg[1])
    image_gq, text_gq = compact(to_lanes(ia[4])), compact(to_lanes(ta[4]))
    sums = lax.psum((ia[1], ia[2], ta[1], ta[2]), every)

    def qkv_grads(cfg, first, wq, gq, yk, yv, mixed):
        heads, flip = cfg[1], cfg[2]
        pair = (lambda left, right: tn(right, left)) if flip else tn
        queries = (into(first, wq, flip).astype(BF16).astype(F32) * SCALE).astype(BF16)
        q_part = pair(first, gq)
        axis = 0 if flip else 1
        k_part = jnp.concatenate([pair(yk[h], queries[:, h * HEAD : (h + 1) * HEAD]) for h in range(heads)], axis=axis)
        v_part = jnp.concatenate([pair(yv[h], mixed[:, h * HEAD : (h + 1) * HEAD]) for h in range(heads)], axis=axis)
        return jnp.stack([q_part, k_part, v_part])

    image_qkv_grad = jnp.transpose(qkv_grads(image_cfg, image_first, image_q[0], image_gq, image_yk, image_yv, ib[1]), (2, 0, 1))
    text_qkv_grad = jnp.transpose(qkv_grads(text_cfg, text_first, text_q[0], text_gq, text_yk, text_yv, tb[1]), (1, 0, 2))
    return (
        image_block, ia[0], image_qkv_grad, ib[2], ib[3], ib[4],
        jnp.concatenate([sums[0], ib[6][0], ib[6][1]], axis=0),
        jnp.concatenate([sums[1], ib[7][0], ib[7][1]], axis=0),
        ib[5],
        text_block, ta[0], text_qkv_grad, tb[2], tb[3], tb[4],
        jnp.concatenate([sums[2], tb[6][0], tb[6][1]], axis=0),
        jnp.concatenate([sums[3], tb[7][0], tb[7][1]], axis=0),
        tb[5],
        scale_grad.reshape(1), loss.reshape(1),
    )


def solution(mesh):
    towers, batches, tensors = (mesh.shape[a] for a in ("tower", "batch", "tensor"))
    fine = Mesh(mesh.devices.reshape(towers, batches // 2, 2, tensors // 2, 2), ("x", "zh", "zb", "y", "c"))
    rows = P(("x", "zh", "zb", "y", "c"), None)
    lanes = ("y", "c")
    weights = (P(None, None, lanes), P(lanes, None), P(None, lanes), P(lanes, None))
    tower_in = (rows, P(), P()) + weights + (P(),)
    tower_out = (rows, rows) + weights + (P(), P(), P())
    return jax.shard_map(
        per_device,
        mesh=fine,
        in_specs=tower_in + tower_in + (P(("x", "zh", "zb")), P()),
        out_specs=tower_out + tower_out + (P(), P()),
        check_vma=False,
    )
```

time: 1140 us -> 685 us (0.60)
  blocking collectives: 452 us -> 40.8 us
  waiting for transfers between devices: 298 us -> 105 us
  matrix products: 126 us -> 291 us
  local copies, waits for them, and re-layouts: 161 us -> 121 us
  starting transfers between devices: 18.7 us -> 52.4 us
  between operations: 21.7 us -> 10 us
    unnamed x5 -> x0, blocking collectives: 294 us -> none
    psum x2 -> x0, waiting for transfers between devices: 242 us -> none  [the longest x1 242 us: per_device(): lax.psum(image_members + text_members + objective_members, ('tower', 'bat...]
    dot_general x48 -> x217, matrix products: 118 us -> 291 us  [the longest x107 139 us: nn(): lax.dot_general(a, b, (((1,), (0,)), ((), ())), preferred_element_type=F32)]
    all_to_all x0 -> x11, waiting for transfers between devices: none -> 90.6 us  [the longest x8 80.8 us: to_lanes(): return lax.all_to_all(wide, every, split_axis=0, concat_axis=0, tiled=True)]
    unnamed x321 -> x832, local copies, waits for them, and re-layouts: 104 us -> 19.5 us
    all_gather x2 -> x0, blocking collectives: 64.4 us -> none  [the longest x1 33.3 us: per_device(): lax.all_gather(text_unit, ('tower', 'batch'), axis=0, tiled=True)]
    all_gather x8 -> x0, waiting for transfers between devices: 55.6 us -> none  [spread_rows(): return lax.all_gather(values, 'tensor', axis=0, tiled=True)]
    psum x3 -> x1, blocking collectives: 93.4 us -> 40.8 us  [per_device(): sums = lax.psum((ia[1], ia[2], ta[1], ta[2]), every)]
  transfers between devices with their start and end apart: 18 -> 35, of which waited for: 6 -> 11; matrix products, arithmetic and copies ran while one was open for 22% -> 46% of each run, Pallas kernels for 0% -> 0%
where the time goes in v1:
time: 685 us; the launch traced here: 676 us
  matrix products  291 us (42%)
  local copies, waits for them, and re-layouts  121 us (18%)
  waiting for transfers between devices  105 us (15%)
  other arithmetic  54.9 us (8%)
  starting transfers between devices  52.4 us (8%)
  blocking collectives  40.8 us (6%)
  between operations  10 us (1%)
    dot_general x107, matrix products, nn(): lax.dot_general(a, b, (((1,), (0,)), ((), ())), preferred_element_type=F32)  139 us
    dot_general x67, matrix products, nt(): lax.dot_general(a, b, (((1,), (1,)), ((), ())), preferred_element_type=F32)  90.5 us
    all_to_all x8, waiting for transfers between devices, to_lanes(): return lax.all_to_all(wide, every, split_axis=0, concat_axis=0, tiled=True)  80.8 us
    psum x1, blocking collectives, per_device(): sums = lax.psum((ia[1], ia[2], ta[1], ta[2]), every)  40.8 us
    dot_general x25, matrix products, tn(): lax.dot_general(a, b, (((0,), (0,)), ((), ())), preferred_element_type=F32)  30.9 us
    all_to_all x8, starting transfers between devices, to_lanes(): return lax.all_to_all(wide, every, split_axis=0, concat_axis=0, tiled=True)  24.5 us
    reshape x8, local copies, waits for them, and re-layouts, bulk(): middle = middle + nn(mix.astype(BF16).reshape(rows, heads * HEAD), wo[s])  23.4 us
    unnamed x832, local copies, waits for them, and re-layouts  19.5 us
  transfers between devices with their start and end apart: 35, of which 11 were waited for; matrix products, arithmetic and copies ran while one was open for 46% of the time, Pallas kernels for 0%

profile of v1, /device:TPU:0, one launch (start us, length us, event | category | flops | bytes accessed | tf_op | source)
XLA Modules:
  0.0 675.7 jit_solution(2663560167282268886)
XLA Ops:
  1.2 2.6 collective-permute-start
  11.8 5.0 all-to-all-start.6
  51.2 2.4 fusion.50
  56.3 2.4 fusion.577
  95.9 2.5 fusion.617
  99.2 5.7 all-to-all-start.2
  107.4 2.5 fusion.9
  112.7 5.3 all-to-all-done.2
  151.6 3.4 fusion.155
  156.7 3.0 convolution_add_fusion.4
  159.7 5.0 collective-permute-done.19
  166.2 9.7 %collective-permute-done.18 = bf16[512,512]{1,0:T(8,128)(2,1)} collective-permute-done((bf16[512,512]{1,0:T(8,128)(2,1)}, bf16[512,512]{1,0:T(8,128)(2,1)}, u32[]{:S(2)}, u32[]{:S(2)}) %collective-permute-start.18) | collective-permute-done | bytes 524320 | tf_op jit(solution)/shard_map/ppermute | solution.py:274
  177.4 3.6 fusion.8
  210.1 2.4 fusion.52
  212.5 2.4 fusion.51
  219.5 14.8 %reshape.663 = bf16[300,192]{1,0:T(8,128)(2,1)} reshape(bf16[6,50,3,64]{3,2,1,0:T(4,128)(2,1)} %copy.219) | data formatting | bytes 230400 | tf_op jit(solution)/shard_map/reshape | solution.py:154
  244.3 3.2 fusion.21
  280.3 2.7 all-to-all-start
  294.3 4.0 fusion.156
  298.3 4.2 convolution_add_fusion.9
  302.6 4.5 fusion.10
  307.1 4.1 fusion.23
  311.2 4.6 all-to-all-done
  370.1 2.6 fusion.614
  372.8 3.9 convolution_add_fusion.16
  376.7 3.8 convolution_add_fusion.15
  380.5 4.6 multiply_reduce_fusion.6
  408.4 2.7 convolution_add_fusion.22
  411.1 2.8 convolution_add_fusion.21
  414.0 3.4 multiply_reduce_fusion.14
  449.5 3.5 all-to-all-start.7
  478.6 2.9 fusion.132
  481.6 3.4 fusion.125
  485.6 40.8 %all-reduce.3 = (f32[1,768]{1,0:T(1,128)S(1)}, f32[1,768]{1,0:T(1,128)}, f32[1,512]{1,0:T(1,128)}, f32[1,512]{1,0:T(1,128)}) all-reduce(f32[1,768]{1,0:T(1,128)S(1)} %broadcast_in_dim.415, f32[1,768]{1,0:T(1,128)S(1)} %broadcast_in_dim.418, ...), channel_id=1, replica_groups=mesh['x'=2,'zh'=2,'zb'=2,'y'=2,'c'=2] {'x','zh','zb','y','c'}, use_global_device_ids=true, to_apply=%region_56.59 | all-reduce | flops 2560 | bytes 20480 | tf_op jit(solution)/shard_map/psum | solution.py:332
  527.7 4.9 all-to-all-start.10
  533.3 6.6 all-to-all-done.10
  540.7 2.7 all-to-all-start.1
  544.0 7.6 %all-to-all-done.1 = bf16[32,8,192]{2,1,0:T(8,128)(2,1)S(1)} async-done(((bf16[32,8,192]{2,1,0:T(8,128)(2,1)}), bf16[32,8,192]{2,1,0:T(8,128)(2,1)S(1)}, u32[]{:S(2)}, u32[]{:S(2)}) %all-to-all-start.1) | async-done | bytes 98336 | tf_op jit(solution)/shard_map/all_to_all | solution.py:297
  552.3 2.6 all-to-all-start.5
  555.5 7.6 %all-to-all-done.5 = bf16[32,8,192]{2,1,0:T(8,128)(2,1)S(1)} async-done(((bf16[32,8,192]{2,1,0:T(8,128)(2,1)}), bf16[32,8,192]{2,1,0:T(8,128)(2,1)S(1)}, u32[]{:S(2)}, u32[]{:S(2)}) %all-to-all-start.5) | async-done | bytes 98336 | tf_op jit(solution)/shard_map/all_to_all | solution.py:297
  564.0 2.7 all-to-all-start.9
  573.1 9.5 %all-to-all-done.9 = bf16[32,16,512]{2,1,0:T(8,128)(2,1)S(1)} async-done(((bf16[32,16,512]{2,1,0:T(8,128)(2,1)}), bf16[32,16,512]{2,1,0:T(8,128)(2,1)S(1)}, u32[]{:S(2)}, u32[]{:S(2)}) %all-to-all-start.9) | async-done | bytes 524320 | tf_op jit(solution)/shard_map/all_to_all | solution.py:297
  583.5 2.6 all-to-all-start.8
  595.0 7.0 %all-to-all-done.8 = bf16[32,16,512]{2,1,0:T(8,128)(2,1)S(1)} async-done(((bf16[32,16,512]{2,1,0:T(8,128)(2,1)}), bf16[32,16,512]{2,1,0:T(8,128)(2,1)S(1)}, u32[]{:S(2)}, u32[]{:S(2)}) %all-to-all-start.8) | async-done | bytes 524320 | tf_op jit(solution)/shard_map/all_to_all | solution.py:297
  603.2 2.7 all-to-all-start.4
  616.5 19.4 %all-to-all-done.4 = bf16[32,24,768]{2,1,0:T(8,128)(2,1)S(1)} async-done(((bf16[32,24,768]{2,1,0:T(8,128)(2,1)}), bf16[32,24,768]{2,1,0:T(8,128)(2,1)S(1)}, u32[]{:S(2)}, u32[]{:S(2)}) %all-to-all-start.4) | async-done | bytes 1179680 | tf_op jit(solution)/shard_map/all_to_all | solution.py:297
  637.0 2.9 all-to-all-start.3
  646.9 22.9 %all-to-all-done.3 = bf16[32,24,768]{2,1,0:T(8,128)(2,1)S(1)} async-done(((bf16[32,24,768]{2,1,0:T(8,128)(2,1)}), bf16[32,24,768]{2,1,0:T(8,128)(2,1)S(1)}, u32[]{:S(2)}, u32[]{:S(2)}) %all-to-all-start.3) | async-done | bytes 1179680 | tf_op jit(solution)/shard_map/all_to_all | solution.py:297
  (1334 shorter events, 389.4 us)
Async XLA Ops:
  0.7 361.8 %copy-start = (bf16[768,512]{1,0:T(8,128)(2,1)S(1)}, bf16[768,512]{1,0:T(8,128)(2,1)}, u32[]{:S(2)}) copy-start(bf16[768,512]{1,0:T(8,128)(2,1)} %param.33) | copy-start | bytes 2359300
  0.7 180.3 %collective-permute-start.2 = (bf16[3,192,768]{2,1,0:T(8,128)(2,1)}, bf16[3,192,768]{2,1,0:T(8,128)(2,1)}, u32[]{:S(2)}, u32[]{:S(2)}) collective-permute-start(bf16[3,192,768]{2,1,0:T(8,128)(2,1)} %bitcast.603), channel_id=1, source_target_pairs={{0,1},{1,0},{2,3},{3,2},{4,5},{5,4},{6,7},{7,6},{8,9},{9,8},{10,11... | collective-permute-start | bytes 2654216 | tf_op jit(solution)/shard_map/ppermute | solution.py:275
  1.2 194.6 %collective-permute-start = (bf16[3,192,768]{2,1,0:T(8,128)(2,1)}, bf16[3,192,768]{2,1,0:T(8,128)(2,1)}, u32[]{:S(2)}, u32[]{:S(2)}) collective-permute-start(bf16[3,192,768]{2,1,0:T(8,128)(2,1)} %bitcast.604), channel_id=1, source_target_pairs={{0,2},{2,0},{1,3},{3,1},{4,6},{6,4},{5,7},{7,5},{8,10},{10,8},{9,1... | collective-permute-start | bytes 2654216 | tf_op jit(solution)/shard_map/ppermute | solution.py:274
  3.8 234.1 %collective-permute-start.3 = (bf16[192,768]{1,0:T(8,128)(2,1)}, bf16[192,768]{1,0:T(8,128)(2,1)}, u32[]{:S(2)}, u32[]{:S(2)}) collective-permute-start(bf16[192,768]{1,0:T(8,128)(2,1)} %param.30), channel_id=1, source_target_pairs={{0,1},{1,0},{2,3},{3,2},{4,5},{5,4},{6,7},{7,6},{8,9},{9,8},{10,11... | collective-permute-start | bytes 884744 | tf_op jit(solution)/shard_map/ppermute | solution.py:275
  4.0 91.9 %collective-permute-start.15 = (bf16[128,512]{1,0:T(8,128)(2,1)}, bf16[128,512]{1,0:T(8,128)(2,1)}, u32[]{:S(2)}, u32[]{:S(2)}) collective-permute-start(bf16[128,512]{1,0:T(8,128)(2,1)} %param.38), channel_id=1, source_target_pairs={{0,1},{1,0},{2,3},{3,2},{4,5},{5,4},{6,7},{7,6},{8,9},{9,8},{10,11... | collective-permute-start | bytes 393224 | tf_op jit(solution)/shard_map/ppermute | solution.py:275
  4.3 61.6 %collective-permute-start.14 = (bf16[3,512,128]{2,1,0:T(8,128)(2,1)}, bf16[3,512,128]{2,1,0:T(8,128)(2,1)}, u32[]{:S(2)}, u32[]{:S(2)}) collective-permute-start(bf16[3,512,128]{2,1,0:T(8,128)(2,1)} %bitcast.588), channel_id=1, source_target_pairs={{0,1},{1,0},{2,3},{3,2},{4,5},{5,4},{6,7},{7,6},{8,9},{9,8},{10,11... | collective-permute-start | bytes 1179656 | tf_op jit(solution)/shard_map/ppermute | solution.py:275
  11.8 86.6 %all-to-all-start.6 = ((bf16[32,8,512]{2,1,0:T(8,128)(2,1)}), bf16[32,8,512]{2,1,0:T(8,128)(2,1)}, u32[]{:S(2)}, u32[]{:S(2)}) async-start(bf16[32,8,512]{2,1,0:T(8,128)(2,1)} %broadcast_in_dim.423), calls=%async_computation.6 | async-start | bytes 524288 | tf_op jit(solution)/shard_map/all_to_all | solution.py:290
  25.5 214.4 %copy-start.179 = (s32[24]{0:T(128)}, s32[24]{0:T(128)S(1)}, u32[]{:S(2)}) copy-start(s32[24]{0:T(128)S(1)} %add_bitcast_fusion) | copy-start | bytes 292
  25.7 114.1 %copy-start.170 = (s32[16]{0:T(128)}, s32[16]{0:T(128)S(1)}, u32[]{:S(2)}) copy-start(s32[16]{0:T(128)S(1)} %iota_and_fusion.2) | copy-start | bytes 196
  25.7 114.1 %copy-start.173 = (s32[16]{0:T(128)}, s32[16]{0:T(128)S(1)}, u32[]{:S(2)}) copy-start(s32[16]{0:T(128)S(1)} %broadcast_add_fusion.1) | copy-start | bytes 196
  25.7 114.1 %copy-start.176 = (pred[16]{0:T(512)(128)(4,1)}, pred[16]{0:T(512)(128)(4,1)S(1)}, u32[]{:S(2)}) copy-start(pred[16]{0:T(512)(128)(4,1)S(1)} %compare_and_fusion.1) | copy-start | bytes 52
  26.0 32.7 %copy-start.36 = (bf16[462,128]{1,0:T(8,128)(2,1)}, bf16[462,128]{1,0:T(8,128)(2,1)S(1)}, u32[]{:S(2)}) copy-start(bf16[462,128]{1,0:T(8,128)(2,1)S(1)} %convolution_convert_fusion.31) | copy-start | bytes 354820
  65.9 12.8 %collective-permute-start.12 = (bf16[3,512,128]{2,1,0:T(8,128)(2,1)S(1)}, bf16[3,512,128]{2,1,0:T(8,128)(2,1)S(1)}, u32[]{:S(2)}, u32[]{:S(2)}) collective-permute-start(bf16[3,512,128]{2,1,0:T(8,128)(2,1)S(1)} %bitcast.597), channel_id=1, source_target_pairs={{0,2},{2,0},{1,3},{3,1},{4,6},{6,4},{5,7},{7,5},{8,10},{10,8},{9,1... | collective-permute-start | bytes 1179656 | tf_op jit(solution)/shard_map/ppermute | solution.py:274
  78.7 28.5 %collective-permute-start.13 = (bf16[128,512]{1,0:T(8,128)(2,1)}, bf16[128,512]{1,0:T(8,128)(2,1)}, u32[]{:S(2)}, u32[]{:S(2)}) collective-permute-start(bf16[128,512]{1,0:T(8,128)(2,1)} %param.38), channel_id=1, source_target_pairs={{0,2},{2,0},{1,3},{3,1},{4,6},{6,4},{5,7},{7,5},{8,10},{10,8},{9,1... | collective-permute-start | bytes 393224 | tf_op jit(solution)/shard_map/ppermute | solution.py:274
  95.8 53.7 %collective-permute-start.21 = (bf16[512,512]{1,0:T(8,128)(2,1)}, bf16[512,512]{1,0:T(8,128)(2,1)}, u32[]{:S(2)}, u32[]{:S(2)}) collective-permute-start(bf16[512,512]{1,0:T(8,128)(2,1)} %param.40), channel_id=1, source_target_pairs={{0,1},{1,0},{2,3},{3,2},{4,5},{5,4},{6,7},{7,6},{8,9},{9,8},{10,11... | collective-permute-start | bytes 1572872 | tf_op jit(solution)/shard_map/ppermute | solution.py:275
  99.2 18.8 %all-to-all-start.2 = ((bf16[32,8,768]{2,1,0:T(8,128)(2,1)}), bf16[32,8,768]{2,1,0:T(8,128)(2,1)}, u32[]{:S(2)}, u32[]{:S(2)}) async-start(bf16[32,8,768]{2,1,0:T(8,128)(2,1)} %broadcast_in_dim.411), calls=%async_computation.2 | async-start | bytes 786432 | tf_op jit(solution)/shard_map/all_to_all | solution.py:290
  107.2 13.8 %collective-permute-start.16 = (bf16[3,512,128]{2,1,0:T(8,128)(2,1)}, bf16[3,512,128]{2,1,0:T(8,128)(2,1)}, u32[]{:S(2)}, u32[]{:S(2)}) collective-permute-start(bf16[3,512,128]{2,1,0:T(8,128)(2,1)} %copy-done.31), channel_id=1, source_target_pairs={{0,1},{1,0},{2,3},{3,2},{4,5},{5,4},{6,7},{7,6},{8,9},{9,8},{10,11... | collective-permute-start | bytes 1179656 | tf_op jit(solution)/shard_map/ppermute | solution.py:275
  121.0 19.1 %collective-permute-start.17 = (bf16[128,512]{1,0:T(8,128)(2,1)}, bf16[128,512]{1,0:T(8,128)(2,1)}, u32[]{:S(2)}, u32[]{:S(2)}) collective-permute-start(bf16[128,512]{1,0:T(8,128)(2,1)} %collective-permute-done.13), channel_id=1, source_target_pairs={{0,1},{1,0},{2,3},{3,2},{4,5},{5,4},{6,7},{7,6},{8,9},{9,8},{10,11... | collective-permute-start | bytes 393224 | tf_op jit(solution)/shard_map/ppermute | solution.py:275
  140.1 11.0 %collective-permute-start.20 = (bf16[512,512]{1,0:T(8,128)(2,1)}, bf16[512,512]{1,0:T(8,128)(2,1)}, u32[]{:S(2)}, u32[]{:S(2)}) collective-permute-start(bf16[512,512]{1,0:T(8,128)(2,1)} %param.39), channel_id=1, source_target_pairs={{0,1},{1,0},{2,3},{3,2},{4,5},{5,4},{6,7},{7,6},{8,9},{9,8},{10,11... | collective-permute-start | bytes 1572872 | tf_op jit(solution)/shard_map/ppermute | solution.py:275
  149.6 15.1 %collective-permute-start.19 = (bf16[512,512]{1,0:T(8,128)(2,1)}, bf16[512,512]{1,0:T(8,128)(2,1)}, u32[]{:S(2)}, u32[]{:S(2)}) collective-permute-start(bf16[512,512]{1,0:T(8,128)(2,1)} %param.40), channel_id=1, source_target_pairs={{0,2},{2,0},{1,3},{3,1},{4,6},{6,4},{5,7},{7,5},{8,10},{10,8},{9,1... | collective-permute-start | bytes 1572872 | tf_op jit(solution)/shard_map/ppermute | solution.py:274
  151.1 24.8 %collective-permute-start.18 = (bf16[512,512]{1,0:T(8,128)(2,1)}, bf16[512,512]{1,0:T(8,128)(2,1)}, u32[]{:S(2)}, u32[]{:S(2)}) collective-permute-start(bf16[512,512]{1,0:T(8,128)(2,1)} %param.39), channel_id=1, source_target_pairs={{0,2},{2,0},{1,3},{3,1},{4,6},{6,4},{5,7},{7,5},{8,10},{10,8},{9,1... | collective-permute-start | bytes 1572872 | tf_op jit(solution)/shard_map/ppermute | solution.py:274
  164.7 75.1 %collective-permute-start.1 = (bf16[192,768]{1,0:T(8,128)(2,1)S(1)}, bf16[192,768]{1,0:T(8,128)(2,1)}, u32[]{:S(2)}, u32[]{:S(2)}) collective-permute-start(bf16[192,768]{1,0:T(8,128)(2,1)S(1)} %copy-done.14), channel_id=1, source_target_pairs={{0,2},{2,0},{1,3},{3,1},{4,6},{6,4},{5,7},{7,5},{8,10},{10,8},{9,1... | collective-permute-start | bytes 884744 | tf_op jit(solution)/shard_map/ppermute | solution.py:274
  175.9 71.5 %collective-permute-start.7 = (bf16[768,768]{1,0:T(8,128)(2,1)}, bf16[768,768]{1,0:T(8,128)(2,1)}, u32[]{:S(2)}, u32[]{:S(2)}) collective-permute-start(bf16[768,768]{1,0:T(8,128)(2,1)} %param.32), channel_id=1, source_target_pairs={{0,2},{2,0},{1,3},{3,1},{4,6},{6,4},{5,7},{7,5},{8,10},{10,8},{9,1... | collective-permute-start | bytes 3538952 | tf_op jit(solution)/shard_map/ppermute | solution.py:274
  181.0 66.8 %collective-permute-start.6 = (bf16[768,768]{1,0:T(8,128)(2,1)}, bf16[768,768]{1,0:T(8,128)(2,1)}, u32[]{:S(2)}, u32[]{:S(2)}) collective-permute-start(bf16[768,768]{1,0:T(8,128)(2,1)} %param.31), channel_id=1, source_target_pairs={{0,2},{2,0},{1,3},{3,1},{4,6},{6,4},{5,7},{7,5},{8,10},{10,8},{9,1... | collective-permute-start | bytes 3538952 | tf_op jit(solution)/shard_map/ppermute | solution.py:274
  195.8 48.0 %collective-permute-start.23 = (bf16[512,512]{1,0:T(8,128)(2,1)}, bf16[512,512]{1,0:T(8,128)(2,1)}, u32[]{:S(2)}, u32[]{:S(2)}) collective-permute-start(bf16[512,512]{1,0:T(8,128)(2,1)} %collective-permute-done.19), channel_id=1, source_target_pairs={{0,1},{1,0},{2,3},{3,2},{4,5},{5,4},{6,7},{7,6},{8,9},{9,8},{10,11... | collective-permute-start | bytes 1572872 | tf_op jit(solution)/shard_map/ppermute | solution.py:275
  218.6 37.1 %copy-start.303 = (f32[24]{0:T(128)}, f32[24]{0:T(128)S(1)}, u32[]{:S(2)}) copy-start(f32[24]{0:T(128)S(1)} %get-tuple-element.150) | copy-start | bytes 292
  218.6 41.5 %copy-start.93 = (f32[24,300]{1,0:T(8,128)}, f32[24,300]{1,0:T(8,128)S(1)}, u32[]{:S(2)}) copy-start(f32[24,300]{1,0:T(8,128)S(1)} %get-tuple-element.151) | copy-start | bytes 86404
  237.9 6.3 collective-permute-start.22
  239.8 8.2 %collective-permute-start.4 = (bf16[3,192,768]{2,1,0:T(8,128)(2,1)}, bf16[3,192,768]{2,1,0:T(8,128)(2,1)}, u32[]{:S(2)}, u32[]{:S(2)}) collective-permute-start(bf16[3,192,768]{2,1,0:T(8,128)(2,1)} %collective-permute-done), channel_id=1, source_target_pairs={{0,1},{1,0},{2,3},{3,2},{4,5},{5,4},{6,7},{7,6},{8,9},{9,8},{10,11... | collective-permute-start | bytes 2654216 | tf_op jit(solution)/shard_map/ppermute | solution.py:275
  243.7 50.6 %collective-permute-start.9 = (bf16[768,768]{1,0:T(8,128)(2,1)}, bf16[768,768]{1,0:T(8,128)(2,1)}, u32[]{:S(2)}, u32[]{:S(2)}) collective-permute-start(bf16[768,768]{1,0:T(8,128)(2,1)} %param.32), channel_id=1, source_target_pairs={{0,1},{1,0},{2,3},{3,2},{4,5},{5,4},{6,7},{7,6},{8,9},{9,8},{10,11... | collective-permute-start | bytes 3538952 | tf_op jit(solution)/shard_map/ppermute | solution.py:275
  244.2 50.2 %collective-permute-start.8 = (bf16[768,768]{1,0:T(8,128)(2,1)}, bf16[768,768]{1,0:T(8,128)(2,1)}, u32[]{:S(2)}, u32[]{:S(2)}) collective-permute-start(bf16[768,768]{1,0:T(8,128)(2,1)} %param.31), channel_id=1, source_target_pairs={{0,1},{1,0},{2,3},{3,2},{4,5},{5,4},{6,7},{7,6},{8,9},{9,8},{10,11... | collective-permute-start | bytes 3538952 | tf_op jit(solution)/shard_map/ppermute | solution.py:275
  247.4 30.7 %collective-permute-start.5 = (bf16[192,768]{1,0:T(8,128)(2,1)}, bf16[192,768]{1,0:T(8,128)(2,1)S(1)}, u32[]{:S(2)}, u32[]{:S(2)}) collective-permute-start(bf16[192,768]{1,0:T(8,128)(2,1)} %collective-permute-done.1), channel_id=1, source_target_pairs={{0,1},{1,0},{2,3},{3,2},{4,5},{5,4},{6,7},{7,6},{8,9},{9,8},{10,11... | collective-permute-start | bytes 884744 | tf_op jit(solution)/shard_map/ppermute | solution.py:275
  247.8 59.3 %collective-permute-start.11 = (bf16[768,768]{1,0:T(8,128)(2,1)}, bf16[768,768]{1,0:T(8,128)(2,1)}, u32[]{:S(2)}, u32[]{:S(2)}) collective-permute-start(bf16[768,768]{1,0:T(8,128)(2,1)} %collective-permute-done.7), channel_id=1, source_target_pairs={{0,1},{1,0},{2,3},{3,2},{4,5},{5,4},{6,7},{7,6},{8,9},{9,8},{10,11... | collective-permute-start | bytes 3538952 | tf_op jit(solution)/shard_map/ppermute | solution.py:275
  247.9 59.2 %collective-permute-start.10 = (bf16[768,768]{1,0:T(8,128)(2,1)}, bf16[768,768]{1,0:T(8,128)(2,1)}, u32[]{:S(2)}, u32[]{:S(2)}) collective-permute-start(bf16[768,768]{1,0:T(8,128)(2,1)} %collective-permute-done.6), channel_id=1, source_target_pairs={{0,1},{1,0},{2,3},{3,2},{4,5},{5,4},{6,7},{7,6},{8,9},{9,8},{10,11... | collective-permute-start | bytes 3538952 | tf_op jit(solution)/shard_map/ppermute | solution.py:275
  280.3 35.4 %all-to-all-start = ((f32[32,8,1280]{2,1,0:T(8,128)}), f32[32,8,1280]{2,1,0:T(8,128)S(1)}, u32[]{:S(2)}, u32[]{:S(2)}) async-start(f32[32,8,1280]{2,1,0:T(8,128)} %broadcast_in_dim.409), calls=%async_computation | async-start | bytes 2621440 | tf_op jit(solution)/shard_map/all_to_all | solution.py:290
  449.5 77.5 %all-to-all-start.7 = ((bf16[32,8,128]{2,1,0:T(8,128)(2,1)}), bf16[32,8,128]{2,1,0:T(8,128)(2,1)}, u32[]{:S(2)}, u32[]{:S(2)}) async-start(bf16[32,8,128]{2,1,0:T(8,128)(2,1)} %bitcast.78), calls=%async_computation.7 | async-start | bytes 131072 | tf_op jit(solution)/shard_map/all_to_all | solution.py:297
  481.5 45.5 %copy-start.213 = (bf16[4,8,128]{2,1,0:T(8,128)(2,1)S(1)}, bf16[4,8,128]{2,1,0:T(8,128)(2,1)}, u32[]{:S(2)}) copy-start(bf16[4,8,128]{2,1,0:T(8,128)(2,1)} %get-tuple-element.126) | copy-start | bytes 24580
  481.5 51.0 %copy-start.242 = (f32[192]{0:T(256)S(1)}, f32[192]{0:T(256)}, u32[]{:S(2)}) copy-start(f32[192]{0:T(256)} %copy-done.240) | copy-start | bytes 2308
  481.5 51.0 %copy-start.245 = (f32[192]{0:T(256)S(1)}, f32[192]{0:T(256)}, u32[]{:S(2)}) copy-start(f32[192]{0:T(256)} %copy-done.243) | copy-start | bytes 2308
  481.6 58.4 %copy-start.152 = (bf16[4,8,192]{2,1,0:T(8,128)(2,1)S(1)}, bf16[4,8,192]{2,1,0:T(8,128)(2,1)}, u32[]{:S(2)}) copy-start(bf16[4,8,192]{2,1,0:T(8,128)(2,1)} %get-tuple-element.131) | copy-start | bytes 36868
  485.0 78.1 %copy-start.107 = (bf16[4,16,512]{2,1,0:T(8,128)(2,1)S(1)}, bf16[4,16,512]{2,1,0:T(8,128)(2,1)}, u32[]{:S(2)}) copy-start(bf16[4,16,512]{2,1,0:T(8,128)(2,1)} %get-tuple-element.129) | copy-start | bytes 196612
  527.7 12.3 %all-to-all-start.10 = ((bf16[32,8,128]{2,1,0:T(8,128)(2,1)}), bf16[32,8,128]{2,1,0:T(8,128)(2,1)S(1)}, u32[]{:S(2)}, u32[]{:S(2)}) async-start(bf16[32,8,128]{2,1,0:T(8,128)(2,1)} %bitcast.102), calls=%async_computation.10 | async-start | bytes 131072 | tf_op jit(solution)/shard_map/all_to_all | solution.py:297
  540.7 10.9 %all-to-all-start.1 = ((bf16[32,8,192]{2,1,0:T(8,128)(2,1)}), bf16[32,8,192]{2,1,0:T(8,128)(2,1)S(1)}, u32[]{:S(2)}, u32[]{:S(2)}) async-start(bf16[32,8,192]{2,1,0:T(8,128)(2,1)} %bitcast.45), calls=%async_computation.1 | async-start | bytes 262144 | tf_op jit(solution)/shard_map/all_to_all | solution.py:297
  552.3 10.8 %all-to-all-start.5 = ((bf16[32,8,192]{2,1,0:T(8,128)(2,1)}), bf16[32,8,192]{2,1,0:T(8,128)(2,1)S(1)}, u32[]{:S(2)}, u32[]{:S(2)}) async-start(bf16[32,8,192]{2,1,0:T(8,128)(2,1)} %bitcast.69), calls=%async_computation.5 | async-start | bytes 262144 | tf_op jit(solution)/shard_map/all_to_all | solution.py:297
  564.0 18.6 %all-to-all-start.9 = ((bf16[32,16,512]{2,1,0:T(8,128)(2,1)}), bf16[32,16,512]{2,1,0:T(8,128)(2,1)S(1)}, u32[]{:S(2)}, u32[]{:S(2)}) async-start(bf16[32,16,512]{2,1,0:T(8,128)(2,1)} %bitcast.601), calls=%async_computation.9 | async-start | bytes 1048576 | tf_op jit(solution)/shard_map/all_to_all | solution.py:297
  583.5 18.5 %all-to-all-start.8 = ((bf16[32,16,512]{2,1,0:T(8,128)(2,1)}), bf16[32,16,512]{2,1,0:T(8,128)(2,1)S(1)}, u32[]{:S(2)}, u32[]{:S(2)}) async-start(bf16[32,16,512]{2,1,0:T(8,128)(2,1)} %bitcast.600), calls=%async_computation.8 | async-start | bytes 1048576 | tf_op jit(solution)/shard_map/all_to_all | solution.py:297
  603.2 32.7 %all-to-all-start.4 = ((bf16[32,24,768]{2,1,0:T(8,128)(2,1)}), bf16[32,24,768]{2,1,0:T(8,128)(2,1)S(1)}, u32[]{:S(2)}, u32[]{:S(2)}) async-start(bf16[32,24,768]{2,1,0:T(8,128)(2,1)} %bitcast.60), calls=%async_computation.4 | async-start | bytes 2359296 | tf_op jit(solution)/shard_map/all_to_all | solution.py:297
  637.0 32.8 %all-to-all-start.3 = ((bf16[32,24,768]{2,1,0:T(8,128)(2,1)}), bf16[32,24,768]{2,1,0:T(8,128)(2,1)S(1)}, u32[]{:S(2)}, u32[]{:S(2)}) async-start(bf16[32,24,768]{2,1,0:T(8,128)(2,1)} %bitcast.587), calls=%async_computation.3 | async-start | bytes 2359296 | tf_op jit(solution)/shard_map/all_to_all | solution.py:297
  (403 other events, 2140.3 us)

commit v2 on v1

v2 whole, which is shorter than its diff:
```python
import jax
import jax.numpy as jnp
from jax import lax
from jax.experimental import pallas as pl
from jax.experimental.pallas import tpu as pltpu
from jax.sharding import Mesh, PartitionSpec as P

HEAD = 64
PATCHES = 50
CTX = 77
EPS = 1e-05
F32 = jnp.float32
BF16 = jnp.bfloat16
HIGH = lax.Precision.HIGHEST
SCALE = HEAD**-0.5
SWAP = [(0, 1), (1, 0)]
ONE_KERNEL_ROWS = 256
SLOT_LANES = (0, 2, 1, 3)
VMEM_BYTES = 60 * 1024 * 1024


def nn(a, b):
    return lax.dot_general(a, b, (((1,), (0,)), ((), ())), preferred_element_type=F32)


def nt(a, b):
    return lax.dot_general(a, b, (((1,), (1,)), ((), ())), preferred_element_type=F32)


def tn(a, b):
    return lax.dot_general(a, b, (((0,), (0,)), ((), ())), preferred_element_type=F32)


def exact_nn(a, b):
    return lax.dot_general(
        a, b, (((1,), (0,)), ((), ())), precision=HIGH, preferred_element_type=F32
    )


def exact_tn(a, b):
    return lax.dot_general(
        a, b, (((0,), (0,)), ((), ())), precision=HIGH, preferred_element_type=F32
    )


def iota(shape, dim):
    return lax.broadcasted_iota(jnp.int32, shape, dim)


def norm_parts(v):
    mean = jnp.mean(v, axis=-1, keepdims=True)
    centred = v - mean
    inv = lax.rsqrt(jnp.mean(centred * centred, axis=-1, keepdims=True) + EPS)
    return centred * inv, inv


def norm_back(o, unit, inv, gain):
    scaled = o * gain
    mean_o = jnp.mean(scaled, axis=-1, keepdims=True)
    mean_u = jnp.mean(scaled * unit, axis=-1, keepdims=True)
    back = inv * (scaled - mean_o - unit * mean_u)
    return back, jnp.sum(o * unit, axis=0, keepdims=True), jnp.sum(o, axis=0, keepdims=True)


def sigmoid(v):
    return 1.0 / (1.0 + jnp.exp(-v))


def shape_of(shape, dtype):
    return jax.ShapeDtypeStruct(shape, dtype)


def call(name, body, out_types, args, flops, smem=()):
    flat, tree = jax.tree.flatten(args)
    count = len(flat)

    def kernel(*refs):
        body(jax.tree.unflatten(tree, refs[:count]), refs[count:])

    moved = sum(v.size * v.dtype.itemsize for v in flat)
    spaces = [pltpu.SMEM if any(v is t for t in smem) else pltpu.VMEM for v in flat]
    return pl.pallas_call(
        kernel,
        out_shape=out_types,
        in_specs=[pl.BlockSpec(memory_space=space) for space in spaces],
        compiler_params=pltpu.CompilerParams(vmem_limit_bytes=VMEM_BYTES),
        cost_estimate=pl.CostEstimate(flops=flops, bytes_accessed=moved, transcendentals=0),
        name=name,
    )(*flat)


def fused(name, fn, out_types, args, flops, smem=()):
    def body(ins, outs):
        for ref, value in zip(outs, fn(*ins), strict=True):
            ref[...] = value

    return call(name, body, out_types, args, flops, smem)


def as_ones(mask):
    return jnp.where(mask, 1.0, 0.0)


def head_mask(heads):
    shape = (heads * 8, heads * HEAD)
    return (iota(shape, 0) >> 3) == (iota(shape, 1) >> 6)


def seq_mask(lens, heads, length, rows):
    lens_all = jnp.concatenate([lens[...]] * heads, axis=0)
    shape = (heads * 8, rows)
    low = (iota(shape, 0) & 7) * length
    col = iota(shape, 1)
    return (col >= low) & (col < low + lens_all)


def pick_rows(lens, length, rows):
    shape = (8, rows)
    held = lens[...]
    back = held - 1 if length == CTX else 0
    spot = jnp.where(held > 0, iota((8, 1), 0) * length + back, -1)
    return as_ones(iota(shape, 1) == spot)


def spread_heads(rows, mask, heads):
    return jnp.where(mask, jnp.concatenate([rows.astype(F32)] * heads, axis=0), 0.0)


def fold_heads(rows, mask, heads):
    kept = jnp.where(mask, rows, 0.0)
    total = kept[:8]
    for h in range(1, heads):
        total = total + kept[8 * h : 8 * h + 8]
    return total


class Tower:
    def __init__(self, length, heads, width, rows, seqs, flip):
        self.length, self.heads, self.width, self.rows, self.seqs, self.flip = length, heads, width, rows, seqs, flip
        self.part = heads * HEAD
        self.padded = -(-rows // 16) * 16
        self.piece = -(-self.part // 128) * 128
        self.per_row = width // self.piece

    def into(self, a, w):
        return nt(a, w) if self.flip else nn(a, w)

    def outof(self, a, w):
        return nn(a, w) if self.flip else nt(a, w)

    def through(self, a, w):
        return nn(a, w) if self.flip else nt(a, w)

    def through_back(self, a, w):
        return nt(a, w) if self.flip else nn(a, w)


def lane_rows(tower, small):
    shape = (tower.part, tower.piece)
    wide = nn(small, as_ones(iota(shape, 0) == iota(shape, 1)).astype(BF16))
    empty = jnp.zeros((1, tower.piece), F32)
    rows = []
    for first in (0, tower.per_row):
        ends = range(first, first + tower.per_row)
        rows.append(jnp.concatenate([wide[n : n + 1] if n < tower.seqs else empty for n in ends], axis=1))
    return rows


def fill_spare(rows, spare):
    row = iota(rows.shape, 0)
    for place, value in spare:
        rows = jnp.where(row == place, value, rows)
    return rows


def front_body(tower, groups, ins, outs):
    tokens, gains, shifts, lens, lane, slots = ins
    middle_out, normed_out, key_out, value_out, prob_out, query_out, early_out = outs
    heads = tower.heads
    low_tokens = tokens[...]
    unit, _ = norm_parts(low_tokens.astype(F32))
    normed = (unit * gains[0:1, :] + shifts[0:1, :]).astype(BF16)
    normed_out[...] = normed
    pick = pick_rows(lens, tower.length, tower.padded).astype(BF16)
    middle = nn(pick, low_tokens)
    normed_pick = nn(pick, normed).astype(BF16)
    allowed = seq_mask(lens, heads, tower.length, tower.padded)
    mask = head_mask(heads)
    for s in range(4):
        key = tower.into(normed, slots[s][1]).astype(BF16)
        value = tower.into(normed, slots[s][2]).astype(BF16)
        query = tower.into(normed_pick, slots[s][0]).astype(BF16)
        key_out[s] = key
        value_out[s] = value
        query_out[s] = query
        scores = nt(spread_heads(query, mask, heads).astype(BF16), key) * SCALE
        scores = jnp.where(allowed, scores, -1e9)
        weights = jnp.where(allowed, jnp.exp(scores - jnp.max(scores, axis=-1, keepdims=True)), 0.0)
        total = jnp.sum(weights, axis=-1, keepdims=True)
        prob = weights / jnp.where(total > 0.0, total, 1.0)
        prob_out[s] = prob
        low = prob.astype(BF16)
        mix = fold_heads(nn(low, value), mask, heads).astype(BF16)
        middle = middle + tower.through(mix, slots[s][3])
        halves = lane_rows(tower, mix)
        y = fill_spare(nn(low, normed), ((14, halves[0]), (15, halves[1])))
        block = jnp.concatenate([y, normed_pick.astype(F32)], axis=0).astype(BF16)
        early_out[:, lane[0] ^ SLOT_LANES[s]] = jnp.broadcast_to(block[None], (groups,) + block.shape)
    middle_out[...] = middle.astype(BF16)


def front_types(tower, groups):
    return (
        shape_of((8, tower.width), BF16),
        shape_of((tower.padded, tower.width), BF16),
        shape_of((4, tower.padded, tower.part), BF16),
        shape_of((4, tower.padded, tower.part), BF16),
        shape_of((4, tower.heads * 8, tower.padded), F32),
        shape_of((4, 8, tower.part), BF16),
        shape_of((groups, 4, tower.heads * 8 + 8, tower.width), BF16),
    )


def window(first, last, tower):
    low = first // tower.length * tower.length // 16 * 16
    high = -(-(((last - 1) // tower.length + 1) * tower.length) // 16) * 16
    return low, min(high, tower.padded)


def mix_body(tower, ins, outs):
    tokens, gains, shifts, lens, normed, keys, values, slots = ins
    middle_out, normed_out = outs
    length, heads, rows = tower.length, tower.heads, tower.padded
    tile = 160 if length == CTX else 112
    row = iota((rows, 1), 0)
    low = jnp.zeros((rows, 1), jnp.int32)
    high = jnp.zeros((rows, 1), jnp.int32)
    for n in range(tower.seqs):
        here = (row >= n * length) & (row < (n + 1) * length)
        low = jnp.where(here, n * length, low)
        end = n * length + lens[n : n + 1, :]
        if length == CTX:
            end = jnp.minimum(end, row + 1)
        high = jnp.where(here, end, high)
    spans = [(first, min(first + tile, rows)) for first in range(0, rows, tile)]
    allowed = []
    for first, last in spans:
        start, stop = window(first, last, tower)
        col = iota((last - first, stop - start), 1) + start
        allowed.append((col >= low[first:last]) & (col < high[first:last]))
    held = normed[...]
    middle = tokens[...].astype(F32)
    lane_head = iota((1, tower.part), 1) >> 6
    for s in range(4):
        query = tower.into(held, slots[s][0]).astype(BF16)
        mixes = []
        for (first, last), mask in zip(spans, allowed, strict=True):
            start, stop = window(first, last, tower)
            mine = query[first:last].astype(F32)
            mix = None
            for h in range(heads):
                one = jnp.where(lane_head == h, mine, 0.0).astype(BF16)
                scores = nt(one, keys[s, start:stop, :]) * SCALE
                scores = jnp.where(mask, scores, -1e9)
                weights = jnp.exp(scores - jnp.max(scores, axis=-1, keepdims=True))
                prob = (weights / jnp.sum(weights, axis=-1, keepdims=True)).astype(BF16)
                part = jnp.where(lane_head == h, nn(prob, values[s, start:stop, :]), 0.0)
                mix = part if mix is None else mix + part
            mixes.append(mix)
        middle = middle + tower.through(jnp.concatenate(mixes, axis=0).astype(BF16), slots[s][3])
    middle_out[...] = middle
    unit, _ = norm_parts(middle)
    normed_out[...] = (unit * gains[1:2, :] + shifts[1:2, :]).astype(BF16)


def mlp_body(tower, ins, outs):
    middle, normed, after, slots = ins
    final = middle[...]
    held = normed[...]
    width = tower.width
    for s in range(4):
        pre = nn(held, slots[s][:width, :])
        final = final + nn((pre * sigmoid(1.702 * pre)).astype(BF16), slots[s][width:, :])
    outs[0][...] = final[: tower.rows].astype(BF16)


def mlp_head_forward(tower, middle, gains, shifts, slots, proj):
    width = tower.width
    unit_two, inv_two = norm_parts(middle)
    normed_two = (unit_two * gains[1:2, :] + shifts[1:2, :]).astype(BF16)
    final = middle
    pres, hids = [], []
    for s in range(4):
        pre = nn(normed_two, slots[s][:width, :])
        hid = (pre * sigmoid(1.702 * pre)).astype(BF16)
        final = final + nn(hid, slots[s][width:, :])
        pres.append(pre)
        hids.append(hid)
    unit_head, inv_head = norm_parts(final)
    normed_head = (unit_head * gains[2:3, :] + shifts[2:3, :]).astype(BF16)
    embedding = nn(normed_head, proj[...])
    inv_len = lax.rsqrt(jnp.sum(embedding * embedding, axis=-1, keepdims=True) + 1e-06)
    unit = (embedding * inv_len).astype(BF16)
    return unit, (unit_two, inv_two, normed_two, pres, hids[0], unit_head, inv_head, normed_head, embedding, inv_len)


def mlp_head_backward(tower, grad_unit, kept, gains, slots, proj):
    unit_two, inv_two, normed_two, pres, hid, unit_head, inv_head, normed_head, embedding, inv_len = kept
    width = tower.width
    along = jnp.sum(embedding * grad_unit, axis=-1, keepdims=True)
    grad_emb = (inv_len * grad_unit - inv_len * inv_len * inv_len * embedding * along).astype(BF16)
    proj_grad = tn(normed_head, grad_emb)
    grad_final, gain_2, shift_2 = norm_back(nt(grad_emb, proj[...]), unit_head, inv_head, gains[2:3, :])
    grad_mlp = grad_final.astype(BF16)
    grad_two = None
    for s in range(4):
        gate = sigmoid(1.702 * pres[s])
        slope = gate + 1.702 * pres[s] * gate * (1.0 - gate)
        grad_pre = (nt(grad_mlp, slots[s][width:, :]) * slope).astype(BF16)
        part = nt(grad_pre, slots[s][:width, :])
        grad_two = part if grad_two is None else grad_two + part
        if s == 0:
            down_grad = tn(hid, grad_mlp)
            up_grad = tn(normed_two, grad_pre)
    back, gain_1, shift_1 = norm_back(grad_two, unit_two, inv_two, gains[1:2, :])
    grad_middle = grad_final + back
    gains_grad = jnp.concatenate([gain_1, gain_2], axis=0)
    shifts_grad = jnp.concatenate([shift_1, shift_2], axis=0)
    return grad_middle, up_grad, down_grad, proj_grad, gains_grad, shifts_grad


def total(v):
    return jnp.sum(jnp.sum(v, axis=1, keepdims=True), axis=0, keepdims=True)


def contrast(image_unit, text_unit, logit_scale):
    factor = jnp.exp(logit_scale[...])
    logits = factor * nt(image_unit, text_unit)
    count = logits.shape[0]
    row_top = jnp.max(logits, axis=1, keepdims=True)
    row_lse = row_top + jnp.log(jnp.sum(jnp.exp(logits - row_top), axis=1, keepdims=True))
    col_top = jnp.max(logits, axis=0, keepdims=True)
    col_lse = col_top + jnp.log(jnp.sum(jnp.exp(logits - col_top), axis=0, keepdims=True))
    eye = iota(logits.shape, 0) == iota(logits.shape, 1)
    diag = total(jnp.where(eye, logits, 0.0))
    loss = (0.5 * (total(row_lse) + total(col_lse)) - diag) / count
    grad = 0.5 * (jnp.exp(logits - row_lse) + jnp.exp(logits - col_lse))
    low = jnp.where(eye, grad - 1.0, grad).astype(BF16)
    scale_grad = total(low.astype(F32) * logits)
    grad_image = factor * nn(low, text_unit)
    grad_text = factor * tn(low, image_unit)
    return loss, scale_grad, grad_image, grad_text


def pooled_back(towers, devices, one_hot, place, mids, image, text, logit_scale):
    seqs = towers[0].seqs
    pairs, spread, half = devices * seqs, devices * 8, devices * 4
    own_mids, other_mids = mids
    core = place[0] & 1
    if one_hot:
        pair = iota((pairs, 1), 0)
        device = ((2 * pair + 1) * (65536 // (2 * seqs) + 1)) >> 16
        spot = (device >> 1) * 8 + (pair - device * seqs)
        spot = jnp.where((device & 1) == core, spot, spot + half)
        pick = as_ones(iota((pairs, spread), 1) == spot).astype(BF16)
        split = towers[0].width
        rows = [
            nn(pick, jnp.concatenate([own_mids[:, cut], other_mids[:, cut]], axis=0))
            for cut in (slice(0, split), slice(split, split + towers[1].width))
        ]
        back_shape = (spread, pairs)
        place_back = as_ones(iota(back_shape, 0) == widen(pairs, seqs))
        own_shape = (8, pairs)
        own_row = iota((8, 1), 0)
        pick_mine = as_ones(iota(own_shape, 1) == jnp.where(own_row < seqs, place[0] * seqs + own_row, -1))
    else:
        both = jnp.stack([own_mids, other_mids]).reshape(2, devices // 2, 8, own_mids.shape[-1])
        both = jnp.where(core == 0, both, both[::-1])
        rows = jnp.swapaxes(both, 0, 1).reshape(devices, 8, -1)[:, :seqs].reshape(pairs, -1).astype(F32)
        rows = [rows[:, : towers[0].width], rows[:, towers[0].width :]]
    units, kept = [], []
    for tower, middle, (gains, shifts, slots, proj) in zip(towers, rows, (image, text), strict=True):
        unit, state = mlp_head_forward(tower, middle, gains, shifts, slots, proj)
        units.append(unit)
        kept.append(state)
    loss, scale_grad, grad_image, grad_text = contrast(units[0], units[1], logit_scale)
    results = ()
    for tower, grad, state, (gains, shifts, slots, proj) in zip(towers, (grad_image, grad_text), kept, (image, text), strict=True):
        grad_middle, *rest = mlp_head_backward(tower, grad, state, gains, slots, proj)
        low = grad_middle.astype(BF16)
        if one_hot:
            branch = nn(place_back.astype(BF16), low).astype(BF16)
            own = exact_nn(pick_mine, grad_middle)
        else:
            branch = jnp.pad(low.reshape(devices, seqs, -1), ((0, 0), (0, 8 - seqs), (0, 0))).reshape(spread, -1)
            own = jnp.pad(lax.dynamic_slice(grad_middle, (place[0] * seqs, 0), (seqs, tower.width)), ((0, 8 - seqs), (0, 0)))
        results += (own, branch) + tuple(rest)
    return results + (loss, scale_grad)


def widen(pairs, seqs):
    pair = iota((1, pairs), 1)
    device = ((2 * pair + 1) * (65536 // (2 * seqs) + 1)) >> 16
    return device * 8 + (pair - device * seqs)


def pooled_types(tower, spread, slots, proj):
    width = tower.width
    return (
        shape_of((8, width), F32),
        shape_of((spread, width), BF16),
        shape_of((width, slots[0].shape[0] - width), F32),
        shape_of((slots[0].shape[0] - width, width), F32),
        shape_of(proj.shape, F32),
        shape_of((2, width), F32),
        shape_of((2, width), F32),
    )


def back_body(tower, groups, ins, outs):
    tokens, gains, lens, lane, grad_rows, normed, keys, values, probs, queries, slots = ins
    grad_out, late_out = outs
    heads = tower.heads
    unit, inv = norm_parts(tokens[...].astype(F32))
    mask = head_mask(heads)
    held = normed[...]
    grad_rows = grad_rows[...]
    branch = grad_rows.astype(BF16)
    left, right, y_keys, g_queries = [], [], [], []
    query_side = None
    for s in range(4):
        grad_mixed = tower.through_back(branch, slots[s][3]).astype(BF16)
        spread = spread_heads(grad_mixed, mask, heads).astype(BF16)
        grad_probs = nt(spread, values[s])
        prob = probs[s]
        grad_scores = (prob * (grad_probs - jnp.sum(prob * grad_probs, axis=-1, keepdims=True))).astype(BF16)
        grad_query = (fold_heads(nn(grad_scores, keys[s]), mask, heads) * SCALE).astype(BF16)
        part = tower.outof(grad_query, slots[s][0])
        query_side = part if query_side is None else query_side + part
        wide = (spread_heads(queries[s], mask, heads) * SCALE).astype(BF16)
        left += [grad_scores, prob.astype(BF16)]
        right += [tower.outof(wide, slots[s][1]).astype(BF16), tower.outof(spread, slots[s][2]).astype(BF16)]
        y_keys.append(nn(grad_scores, held))
        g_queries.append(grad_query)
    pick = pick_rows(lens, tower.length, tower.padded)
    grad_one = tn(jnp.concatenate(left, axis=0), jnp.concatenate(right, axis=0))
    grad_one = grad_one + tn(pick.astype(BF16), query_side.astype(BF16))
    back, gain_0, shift_0 = norm_back(grad_one, unit, inv, gains[0:1, :])
    grad_tokens = exact_tn(pick, grad_rows) + back
    grad_out[...] = grad_tokens[: tower.rows].astype(BF16)
    for s in range(4):
        halves = lane_rows(tower, g_queries[s])
        block = fill_spare(y_keys[s], ((6, gain_0), (7, shift_0), (14, halves[0]), (15, halves[1]))).astype(BF16)
        late_out[:, lane[0] ^ SLOT_LANES[s]] = jnp.broadcast_to(block[None], (groups,) + block.shape)


def back_types(tower, groups):
    return (
        shape_of((tower.rows, tower.width), BF16),
        shape_of((groups, 4, tower.heads * 8, tower.width), BF16),
    )


def last_step(tower, devices, one_hot, branch, wq, wo, early, late, gains, shifts):
    heads, part, piece = tower.heads, tower.part, tower.piece
    spread = devices * 8
    lane_head = iota((1, 1, 1, part), 3) >> 6

    def block_rows(block, per, first):
        if not one_hot:
            return block.reshape(devices, per, -1)[:, first : first + 8].reshape(spread, -1)
        shape = (spread, devices * per)
        row = iota((spread, 1), 0)
        return nn(as_ones(iota(shape, 1) == (row >> 3) * per + first + (row & 7)).astype(BF16), block).astype(BF16)

    def spare_rows(block, per, place):
        if not one_hot:
            return block.reshape(devices, per, -1)[:, place]
        shape = (devices, devices * per)
        return nn(as_ones(iota(shape, 1) == iota((devices, 1), 0) * per + place).astype(BF16), block).astype(BF16)

    def sum_rows(block, per, place):
        if not one_hot:
            return jnp.sum(block.reshape(devices, per, -1)[:, place].astype(F32), axis=0, keepdims=True)
        return jnp.sum(spare_rows(block, per, place).astype(F32), axis=0, keepdims=True)

    def small_rows(block, per):
        halves = (spare_rows(block, per, 14), spare_rows(block, per, 15))
        if not one_hot:
            both = jnp.concatenate(halves, axis=1).reshape(devices, -1, piece)[:, :8, :part]
            both = jnp.pad(both[:, : tower.seqs], ((0, 0), (0, 8 - tower.seqs), (0, 0)))
            return both.reshape(spread, part)
        row, col = iota((spread, devices), 0), iota((spread, devices), 1)
        rows = None
        for n in range(tower.seqs):
            here = n % tower.per_row * piece
            one = nn(as_ones((row >> 3 == col) & ((row & 7) == n)).astype(BF16), halves[n // tower.per_row][:, here : here + part])
            rows = one if rows is None else rows + one
        return rows.astype(BF16)

    def by_head(rows, per):
        blocks = per // 8
        wide = jnp.broadcast_to(rows.reshape(devices, 1, 8, part), (devices, blocks, 8, part))
        number = iota((1, blocks, 1, 1), 1)
        return jnp.where(lane_head == number, wide, 0.0).reshape(devices * per, part).astype(BF16)

    def pair(left, right):
        return tn(right, left) if tower.flip else tn(left, right)

    early_per, late_per = heads * 8 + 8, heads * 8
    branch, early, late = branch[...], early[...], late[...]
    first = block_rows(early, early_per, heads * 8)
    queries = tower.into(first, wq[...]).astype(BF16).astype(F32) * SCALE
    grad_mixed = nt(branch, wo[...]).astype(BF16).astype(F32)
    mixes = small_rows(early, early_per)
    grad_queries = small_rows(late, late_per)
    q_part = pair(first, grad_queries)
    k_part = pair(late, by_head(queries, late_per))
    v_part = pair(early, by_head(grad_mixed, early_per))
    out_grad = tn(mixes, branch)
    gains_grad = jnp.concatenate([sum_rows(late, late_per, 6), gains[...]], axis=0)
    shifts_grad = jnp.concatenate([sum_rows(late, late_per, 7), shifts[...]], axis=0)
    return q_part, k_part, v_part, out_grad, gains_grad, shifts_grad


def per_device(
    image_tokens, image_gains, image_shifts, image_qkv, image_out, image_up, image_down, image_proj,
    text_tokens, text_gains, text_shifts, text_qkv, text_out, text_up, text_down, text_proj,
    caption_lengths, logit_scale,
):
    every = ("x", "zh", "zb", "y", "c")
    devices = lax.axis_size(every)
    groups = devices // 4
    lane = lax.axis_index(("y", "c")).astype(jnp.int32).reshape(1)
    me = lax.axis_index(every).astype(jnp.int32).reshape(1)
    seqs = image_tokens.shape[0] // PATCHES
    towers = (
        Tower(PATCHES, image_out.shape[0] // HEAD, image_tokens.shape[1], image_tokens.shape[0], seqs, True),
        Tower(CTX, text_out.shape[0] // HEAD, text_tokens.shape[1], text_tokens.shape[0], seqs, False),
    )
    small = devices * seqs <= ONE_KERNEL_ROWS
    image_lens = jnp.where(iota((8, 1), 0) < seqs, PATCHES, 0)
    own_lens = lax.dynamic_slice(caption_lengths, (lane[0] * seqs,), (seqs,))
    lens = (image_lens, jnp.pad(own_lens, (0, 8 - seqs)).reshape(8, 1))
    gains, shifts = (image_gains, text_gains), (image_shifts, text_shifts)
    tokens = tuple(jnp.pad(v, ((0, t.padded - t.rows), (0, 0))) for t, v in zip(towers, (image_tokens, text_tokens)))

    corner = lax.axis_index(("x", "zb"))

    def gather(quarters):
        mine = lax.dynamic_index_in_dim(quarters, corner, 0, keepdims=False)
        over = lax.ppermute(mine, "y", SWAP)
        wide = jnp.broadcast_to(over[None], quarters.shape)
        across = lax.all_to_all(wide, ("x", "zb"), split_axis=0, concat_axis=0, tiled=True)
        return [quarters, across, lax.ppermute(quarters, "c", SWAP), lax.ppermute(across, "c", SWAP)]

    text_attn = gather(jnp.concatenate([jnp.transpose(text_qkv, (1, 0, 2)), text_out.T[None]], axis=0))
    image_attn = gather(jnp.concatenate([jnp.transpose(image_qkv, (1, 2, 0)), image_out[None]], axis=0))

    def quarter(up, down):
        both = jnp.concatenate([up, down], axis=0)
        return both.reshape(4, both.shape[0] // 4, both.shape[1])

    def joined(slots):
        return [w.reshape(-1, w.shape[-1]) for w in slots]

    image_mlp = joined(gather(quarter(image_up, image_down)))
    text_mlp = joined(gather(quarter(text_up, text_down)))
    attn, mlp = (image_attn, text_attn), (image_mlp, text_mlp)
    names = ("image", "text")

    fronts = [None, None]
    for i in (1, 0):
        fronts[i] = call(
            "front_" + names[i],
            lambda ins, outs, tower=towers[i]: front_body(tower, groups, ins, outs),
            front_types(towers[i], groups),
            (tokens[i], gains[i], shifts[i], lens[i], lane, attn[i]),
            2 * 10**9,
            smem=(lane,),
        )

    def same_core(v):
        wide = jnp.broadcast_to(v[None], (devices // 2,) + v.shape)
        got = lax.all_to_all(wide, ("x", "zh", "zb", "y"), split_axis=0, concat_axis=0, tiled=True)
        got = got.reshape(devices * 4, v.shape[-1])
        return got, lax.ppermute(got, "c", SWAP)

    def swap_all(v):
        got = lax.all_to_all(v.reshape((devices,) + v.shape[2:]), every, split_axis=0, concat_axis=0, tiled=True)
        return got.reshape(-1, v.shape[-1])

    mids = same_core(jnp.concatenate([fronts[0][0], fronts[1][0]], axis=1))
    early = [swap_all(f[6]) for f in fronts]

    mixed = []
    for i in range(2):
        types = (shape_of(tokens[i].shape, F32), shape_of(tokens[i].shape, BF16))
        front = fronts[i]
        args = (tokens[i], gains[i], shifts[i], lens[i], front[1], front[2], front[3], attn[i])
        mixed.append(call("mix_" + names[i], lambda ins, outs, tower=towers[i]: mix_body(tower, ins, outs), types, args, 4 * 10**9))

    projs = (image_proj, text_proj)
    pools = [(gains[i], shifts[i], mlp[i], projs[i]) for i in range(2)]
    scale = logit_scale.reshape(1, 1)
    args = (me, mids, pools[0], pools[1], scale)
    if small:
        types = ()
        for i in range(2):
            types += pooled_types(towers[i], devices * 8, mlp[i], projs[i])
        types += (shape_of((1, 1), F32),) * 2
        pooled = fused("pooled", lambda *v: pooled_back(towers, devices, True, *v), types, args, 10**10, smem=(me,))
    else:
        pooled = pooled_back(towers, devices, False, *args)
    pools = (pooled[:7], pooled[7:14])
    loss, scale_grad = pooled[14:]

    backs, late = [], []
    for i in range(2):
        front = fronts[i]
        args = (tokens[i], gains[i], lens[i], lane, pools[i][0], front[1], front[2], front[3], front[4], front[5], attn[i])
        backs.append(call(
            "back_" + names[i],
            lambda ins, outs, tower=towers[i]: back_body(tower, groups, ins, outs),
            back_types(towers[i], groups), args, 10**9, smem=(lane,),
        ))
        late.append(swap_all(backs[i][1]))

    blocks = []
    for i in range(2):
        types = (shape_of((towers[i].rows, towers[i].width), BF16),)
        after = backs[1][0][:8, :128]
        args = (mixed[i][0], mixed[i][1], after, mlp[i])
        blocks.append(call("mlp_" + names[i], lambda ins, outs, tower=towers[i]: mlp_body(tower, ins, outs), types, args, 8 * 10**9)[0])

    ends = []
    own_q = (image_attn[0][0], text_attn[0][0])
    for i, wo in enumerate((image_out, text_out)):
        tower = towers[i]
        args = (pools[i][1], own_q[i], wo, early[i], late[i], pools[i][5], pools[i][6])
        if small:
            types = (shape_of(own_q[i].shape, F32),) * 3 + (shape_of(wo.shape, F32),) + (shape_of((3, tower.width), F32),) * 2
            ends.append(fused("last_" + names[i], lambda *v, tower=tower: last_step(tower, devices, True, *v), types, args, 10**9))
        else:
            ends.append(last_step(tower, devices, False, *args))

    image_qkv_grad = jnp.transpose(jnp.stack(ends[0][:3]), (2, 0, 1))
    text_qkv_grad = jnp.transpose(jnp.stack(ends[1][:3]), (1, 0, 2))
    results = ()
    for i, qkv_grad in enumerate((image_qkv_grad, text_qkv_grad)):
        own, branch, up_grad, down_grad, proj_grad, _, _ = pools[i]
        results += (blocks[i], backs[i][0], qkv_grad, ends[i][3], up_grad, down_grad, ends[i][4], ends[i][5], proj_grad)
    return results + (scale_grad.reshape(1), loss.reshape(1))


def solution(mesh):
    towers, batches, tensors = (mesh.shape[a] for a in ("tower", "batch", "tensor"))
    fine = Mesh(mesh.devices.reshape(towers, batches // 2, 2, tensors // 2, 2), ("x", "zh", "zb", "y", "c"))
    rows = P(("x", "zh", "zb", "y", "c"), None)
    lanes = ("y", "c")
    weights = (P(None, None, lanes), P(lanes, None), P(None, lanes), P(lanes, None))
    tower_in = (rows, P(), P()) + weights + (P(),)
    tower_out = (rows, rows) + weights + (P(), P(), P())
    return jax.shard_map(
        per_device,
        mesh=fine,
        in_specs=tower_in + tower_in + (P(("x", "zh", "zb")), P()),
        out_specs=tower_out + tower_out + (P(), P()),
        check_vma=False,
    )
```

time: 685 us -> 269 us (0.39)
  matrix products: 291 us -> 0 us
  Pallas kernels: 0 us -> 111 us
  local copies, waits for them, and re-layouts: 121 us -> 19.3 us
  other arithmetic: 54.9 us -> 9.56 us
  blocking collectives: 40.8 us -> 0 us
  waiting for transfers between devices: 105 us -> 77.6 us
  between operations: 10 us -> 1.83 us
    dot_general x217 -> x0, matrix products: 291 us -> none  [the longest x107 139 us: nn(): lax.dot_general(a, b, (((1,), (0,)), ((), ())), preferred_element_type=F32)]
    pallas_call x0 -> x11, Pallas kernels: none -> 111 us  [call(): pl.pallas_call(kernel, out_shape=out_types, in_specs=[pl.BlockSpec(memory...]
    reshape x38 -> x2, local copies, waits for them, and re-layouts: 61.1 us -> 0.68 us  [per_device(): lens = (image_lens, jnp.pad(own_lens, (0, 8 - seqs)).reshape(8, 1))]
    all_to_all x11 -> x9, waiting for transfers between devices: 90.6 us -> 37.6 us  [the longest x4 20.1 us: gather(): lax.all_to_all(wide, ('x', 'zb'), split_axis=0, concat_axis=0, tiled=True)]
    psum x1 -> x0, blocking collectives: 40.8 us -> none  [per_device(): sums = lax.psum((ia[1], ia[2], ta[1], ta[2]), every)]
    ppermute x24 -> x13, waiting for transfers between devices: 14.8 us -> 40.1 us  [the longest x4 34.4 us: gather(): over = lax.ppermute(mine, 'y', SWAP)]
    unnamed x832 -> x53, local copies, waits for them, and re-layouts: 19.5 us -> 7.93 us
    reduce_sum x17 -> x0, other arithmetic: 11.1 us -> none  [the longest x8 6.97 us: norm_parts(): inv = lax.rsqrt(jnp.mean(centred * centred, axis=-1, keepdims=True) + EPS)]
  transfers between devices with their start and end apart: 35 -> 22, of which waited for: 11 -> 13; matrix products, arithmetic and copies ran while one was open for 46% -> 4% of each run, Pallas kernels for 0% -> 39%
where the time goes in v2:
time: 269 us; the launch traced here: 266 us
  Pallas kernels  111 us (41%)
  waiting for transfers between devices  77.6 us (29%)
  starting transfers between devices  47 us (17%)
  local copies, waits for them, and re-layouts  19.3 us (7%)
  other arithmetic  9.56 us (4%)
    pallas_call x11, Pallas kernels, call(): pl.pallas_call(kernel, out_shape=out_types, in_specs=[pl.BlockSpec(memory...  111 us
    ppermute x4, waiting for transfers between devices, gather(): over = lax.ppermute(mine, 'y', SWAP)  34.4 us
    all_to_all x4, waiting for transfers between devices, gather(): lax.all_to_all(wide, ('x', 'zb'), split_axis=0, concat_axis=0, tiled=True)  20.1 us
    all_to_all x4, starting transfers between devices, swap_all(): lax.all_to_all(v.reshape((devices,) + v.shape[2:]), every, split_axis=0,...  16.2 us
    all_to_all x4, starting transfers between devices, gather(): lax.all_to_all(wide, ('x', 'zb'), split_axis=0, concat_axis=0, tiled=True)  16 us
    all_to_all x1, waiting for transfers between devices, same_core(): lax.all_to_all(wide, ('x', 'zh', 'zb', 'y'), split_axis=0, concat_axis=0,...  10.2 us
    unnamed x53, local copies, waits for them, and re-layouts  7.93 us
    ppermute x4, starting transfers between devices, gather(): over = lax.ppermute(mine, 'y', SWAP)  7.74 us
  transfers between devices with their start and end apart: 22, of which 13 were waited for; matrix products, arithmetic and copies ran while one was open for 4% of the time, Pallas kernels for 39%

profile of v2, /device:TPU:0, one launch (start us, length us, event | category | flops | bytes accessed | tf_op | source)
XLA Modules:
  0.0 266.4 jit_solution(10171081480265800837)
XLA Ops:
  0.7 1.1 copy.38
  1.8 1.7 slice_bitcast_fusion.1
  3.5 3.0 %collective-permute-start.3 = (bf16[512,128]{1,0:T(8,128)(2,1)S(1)}, bf16[512,128]{1,0:T(8,128)(2,1)S(1)}, u32[]{:S(2)}, u32[]{:S(2)}) collective-permute-start(bf16[512,128]{1,0:T(8,128)(2,1)S(1)} %get-tuple-element.123), channel_id=1, source_target_pairs={{0,2},{2,0},{1,3},{3,1},{4,6},{6,4},{5,7},{7,5},{8,10},{10,8},{9,1... | collective-permute-start | bytes 393224 | tf_op jit(solution)/shard_map/ppermute | solution.py:552
  6.5 3.5 %collective-permute-done.3 = bf16[512,128]{1,0:T(8,128)(2,1)S(1)} collective-permute-done((bf16[512,128]{1,0:T(8,128)(2,1)S(1)}, bf16[512,128]{1,0:T(8,128)(2,1)S(1)}, u32[]{:S(2)}, u32[]{:S(2)}) %collective-permute-start.3) | collective-permute-done | bytes 131104 | tf_op jit(solution)/shard_map/ppermute | solution.py:552
  10.8 3.9 %all-to-all-start.1 = ((bf16[4,512,128]{2,1,0:T(8,128)(2,1)}), bf16[4,512,128]{2,1,0:T(8,128)(2,1)S(1)}, u32[]{:S(2)}, u32[]{:S(2)}) async-start(bf16[4,512,128]{2,1,0:T(8,128)(2,1)} %broadcast_in_dim.49), calls=%async_computation.1 | async-start | bytes 1048576 | tf_op jit(solution)/shard_map/all_to_all | solution.py:554
  14.9 1.6 collective-permute-start.10
  16.5 5.5 %collective-permute-done.10 = bf16[256,512]{1,0:T(8,128)(2,1)S(1)} collective-permute-done((bf16[256,512]{1,0:T(8,128)(2,1)S(1)}, bf16[256,512]{1,0:T(8,128)(2,1)S(1)}, u32[]{:S(2)}, u32[]{:S(2)}) %collective-permute-start.10) | collective-permute-done | bytes 262176 | tf_op jit(solution)/shard_map/ppermute | solution.py:552
  22.0 1.2 broadcast_in_dim.52
  23.2 3.9 %all-to-all-start.4 = ((bf16[4,256,512]{2,1,0:T(8,128)(2,1)}), bf16[4,256,512]{2,1,0:T(8,128)(2,1)S(1)}, u32[]{:S(2)}, u32[]{:S(2)}) async-start(bf16[4,256,512]{2,1,0:T(8,128)(2,1)} %broadcast_in_dim.52), calls=%async_computation.4 | async-start | bytes 2097152 | tf_op jit(solution)/shard_map/all_to_all | solution.py:554
  27.9 1.4 collective-permute-start
  29.3 5.4 %collective-permute-done = bf16[192,768]{1,0:T(8,128)(2,1)} collective-permute-done((bf16[192,768]{1,0:T(8,128)(2,1)S(1)}, bf16[192,768]{1,0:T(8,128)(2,1)}, u32[]{:S(2)}, u32[]{:S(2)}) %collective-permute-start) | collective-permute-done | bytes 294944 | tf_op jit(solution)/shard_map/ppermute | solution.py:552
  34.7 4.0 %all-to-all-done.4 = bf16[4,256,512]{2,1,0:T(8,128)(2,1)S(1)} async-done(((bf16[4,256,512]{2,1,0:T(8,128)(2,1)}), bf16[4,256,512]{2,1,0:T(8,128)(2,1)S(1)}, u32[]{:S(2)}, u32[]{:S(2)}) %all-to-all-start.4) | async-done | bytes 1048608 | tf_op jit(solution)/shard_map/all_to_all | solution.py:554
  38.7 2.2 broadcast_in_dim.25
  40.9 3.7 %all-to-all-start = ((bf16[4,192,768]{2,1,0:T(8,128)(2,1)}), bf16[4,192,768]{2,1,0:T(8,128)(2,1)S(1)}, u32[]{:S(2)}, u32[]{:S(2)}) async-start(bf16[4,192,768]{2,1,0:T(8,128)(2,1)} %broadcast_in_dim.25), calls=%async_computation | async-start | bytes 2359296 | tf_op jit(solution)/shard_map/all_to_all | solution.py:554
  46.7 1.8 pad.13.refs_0_
  49.4 6.9 %front_text.1 = (bf16[8,512]{1,0:T(8,128)(2,1)}, bf16[464,512]{1,0:T(8,128)(2,1)}, bf16[4,464,128]{2,1,0:T(8,128)(2,1)}, bf16[4,464,128]{2,1,0:T(8,128)(2,1)}, f...) custom-call(bf16[464,512]{1,0:T(8,128)(2,1)} %pad.13.refs_0_, ...), custom_call_target="tpu_custom_call" | custom-call | flops 2000000000 | bytes 2584612 | tf_op jit(solution)/shard_map/front_text/pallas_call | solution.py:82
  56.2 2.8 %all-to-all-done.refs_6_.refs_8_.refs_11_ = bf16[4,192,768]{2,1,0:T(8,128)(2,1)S(1)} async-done(((bf16[4,192,768]{2,1,0:T(8,128)(2,1)}), bf16[4,192,768]{2,1,0:T(8,128)(2,1)S(1)}, u32[]{:S(2)}, u32[]{:S(2)}) %all-to-all-start) | async-done | bytes 1179680 | tf_op jit(solution)/shard_map/all_to_all | solution.py:554
  59.1 4.7 %all-to-all-start.7 = ((bf16[32,24,512]{2,1,0:T(8,128)(2,1)}), bf16[32,24,512]{2,1,0:T(8,128)(2,1)}, u32[]{:S(2)}, u32[]{:S(2)}) async-start(bf16[32,24,512]{2,1,0:T(8,128)(2,1)} %bitcast.69), calls=%async_computation.7 | async-start | bytes 1572864 | tf_op jit(solution)/shard_map/all_to_all | solution.py:590
  63.9 1.2 copy-done.10
  65.2 1.5 copy-done.8
  66.7 1.8 collective-permute-start.7
  68.4 20.0 %collective-permute-done.7 = bf16[384,768]{1,0:T(8,128)(2,1)S(1)} collective-permute-done((bf16[384,768]{1,0:T(8,128)(2,1)S(1)}, bf16[384,768]{1,0:T(8,128)(2,1)S(1)}, u32[]{:S(2)}, u32[]{:S(2)}) %collective-permute-start.7) | collective-permute-done | bytes 589856 | tf_op jit(solution)/shard_map/ppermute | solution.py:552
  88.4 1.6 broadcast_in_dim.51
  90.0 4.5 %all-to-all-start.3 = ((bf16[4,384,768]{2,1,0:T(8,128)(2,1)}), bf16[4,384,768]{2,1,0:T(8,128)(2,1)}, u32[]{:S(2)}, u32[]{:S(2)}) async-start(bf16[4,384,768]{2,1,0:T(8,128)(2,1)} %broadcast_in_dim.51), calls=%async_computation.3 | async-start | bytes 4718592 | tf_op jit(solution)/shard_map/all_to_all | solution.py:554
  97.5 1.7 collective-permute-done.2.refs_8_.refs_10_.refs_13_
  99.2 1.0 copy-done.12
  100.3 8.4 %front_image.1 = (bf16[8,768]{1,0:T(8,128)(2,1)}, bf16[304,768]{1,0:T(8,128)(2,1)}, bf16[4,304,192]{2,1,0:T(8,128)(2,1)}, bf16[4,304,192]{2,1,0:T(8,128)(2,1)}, ...) custom-call(bf16[304,768]{1,0:T(8,128)(2,1)} %pad.12.refs_0_, ...), custom_call_target="tpu_custom_call" | custom-call | flops 2000000000 | bytes 5204004 | tf_op jit(solution)/shard_map/front_image/pallas_call | solution.py:82
  109.4 13.4 %all-to-all-done.3 = bf16[4,384,768]{2,1,0:T(8,128)(2,1)} async-done(((bf16[4,384,768]{2,1,0:T(8,128)(2,1)}), bf16[4,384,768]{2,1,0:T(8,128)(2,1)}, u32[]{:S(2)}, u32[]{:S(2)}) %all-to-all-start.3) | async-done | bytes 2359328 | tf_op jit(solution)/shard_map/all_to_all | solution.py:554
  123.5 4.8 %all-to-all-start.2 = ((bf16[16,8,1280]{2,1,0:T(8,128)(2,1)}), bf16[16,8,1280]{2,1,0:T(8,128)(2,1)S(1)}, u32[]{:S(2)}, u32[]{:S(2)}) async-start(bf16[16,8,1280]{2,1,0:T(8,128)(2,1)} %broadcast_in_dim.50), calls=%async_computation.2 | async-start | bytes 655360 | tf_op jit(solution)/shard_map/all_to_all | solution.py:585
  128.9 10.2 %all-to-all-done.2 = bf16[16,8,1280]{2,1,0:T(8,128)(2,1)S(1)} async-done(((bf16[16,8,1280]{2,1,0:T(8,128)(2,1)}), bf16[16,8,1280]{2,1,0:T(8,128)(2,1)S(1)}, u32[]{:S(2)}, u32[]{:S(2)}) %all-to-all-start.2) | async-done | bytes 327712 | tf_op jit(solution)/shard_map/all_to_all | solution.py:585
  139.0 2.9 %all-to-all-start.5 = ((bf16[32,32,768]{2,1,0:T(8,128)(2,1)}), bf16[32,32,768]{2,1,0:T(8,128)(2,1)S(1)}, u32[]{:S(2)}, u32[]{:S(2)}) async-start(bf16[32,32,768]{2,1,0:T(8,128)(2,1)} %bitcast.61), calls=%async_computation.5 | async-start | bytes 3145728 | tf_op jit(solution)/shard_map/all_to_all | solution.py:590
  143.3 2.1 collective-permute-done.11
  145.4 1.4 collective-permute-done.12
  147.5 20.5 %pooled.1 = (f32[8,768]{1,0:T(8,128)}, bf16[256,768]{1,0:T(8,128)(2,1)}, f32[768,768]{1,0:T(8,128)}, f32[768,768]{1,0:T(8,128)}, f32[768,512]{1,0:T(8,128)}, /*i...) custom-call(s32[1]{0:T(128)} %bitcast.5.refs_0_, ...), custom_call_target="tpu_custom_call" | custom-call | flops 10000000000 | bytes 15628296 | tf_op jit(solution)/shard_map/pooled/pallas_call | solution.py:82
  168.0 18.1 %back_text.1 = (bf16[462,512]{1,0:T(8,128)(2,1)}, bf16[8,4,16,512]{3,2,1,0:T(8,128)(2,1)}) custom-call(bf16[464,512]{1,0:T(8,128)(2,1)} %pad.13.refs_0_, f32[3,512]{1,0:T(4,128)} %refs_1_.11, s32[8,1]{1,0:T(8,128)} %copy.40.refs_3_.refs_2_, s32[1]{0:T(128)} %bitcast.refs_4_.refs_3_, f32[8,512]{1,0:T(8,128)} %get-tuple-element.77.refs_4_, ...), custom_call_target="tpu_custom_call" | custom-call | flops 1000000000 | bytes 4147236 | tf_op jit(solution)/shard_map/back_text/pallas_call | solution.py:82
  186.1 5.8 %all-to-all-start.8 = ((bf16[32,16,512]{2,1,0:T(8,128)(2,1)}), bf16[32,16,512]{2,1,0:T(8,128)(2,1)S(1)}, u32[]{:S(2)}, u32[]{:S(2)}) async-start(bf16[32,16,512]{2,1,0:T(8,128)(2,1)} %bitcast.76), calls=%async_computation.8 | async-start | bytes 1048576 | tf_op jit(solution)/shard_map/all_to_all | solution.py:590
  191.9 8.6 %back_image.1 = (bf16[300,768]{1,0:T(8,128)(2,1)}, bf16[8,4,24,768]{3,2,1,0:T(8,128)(2,1)}) custom-call(bf16[304,768]{1,0:T(8,128)(2,1)} %pad.12.refs_0_, f32[3,768]{1,0:T(4,128)} %refs_1_.10, s32[8,1]{1,0:T(8,128)} %fusion.4.refs_3_.refs_2_, s32[1]{0:T(128)} %bitcast.refs_4_.refs_3_, f32[8,768]{1,0:T(8,128)} %get-tuple-element.84.refs_4_, ...), custom_call_target="tpu_custom_call" | custom-call | flops 1000000000 | bytes 6749220 | tf_op jit(solution)/shard_map/back_image/pallas_call | solution.py:82
  200.5 7.3 %all-to-all-done.8 = bf16[32,16,512]{2,1,0:T(8,128)(2,1)S(1)} async-done(((bf16[32,16,512]{2,1,0:T(8,128)(2,1)}), bf16[32,16,512]{2,1,0:T(8,128)(2,1)S(1)}, u32[]{:S(2)}, u32[]{:S(2)}) %all-to-all-start.8) | async-done | bytes 524320 | tf_op jit(solution)/shard_map/all_to_all | solution.py:590
  207.8 2.7 all-to-all-start.6
  210.5 10.0 %mix_text.1 = (f32[464,512]{1,0:T(8,128)}, bf16[464,512]{1,0:T(8,128)(2,1)}) custom-call(bf16[464,512]{1,0:T(8,128)(2,1)} %pad.13.refs_0_, f32[3,512]{1,0:T(4,128)} %refs_1_.11, f32[3,512]{1,0:T(4,128)} %refs_2_.10, s32[8,1]{1,0:T(8,128)} %copy.40.refs_3_.refs_2_, bf16[464,512]{1,0:T(8,128)(2,1)} %get-tuple-element.78.refs_5_.refs_4_, ...), custom_call_target="tpu_custom_call" | custom-call | flops 4000000000 | bytes 4010016 | tf_op jit(solution)/shard_map/mix_text/pallas_call | solution.py:82
  220.5 13.6 %mix_image.1 = (f32[304,768]{1,0:T(8,128)}, bf16[304,768]{1,0:T(8,128)(2,1)}) custom-call(bf16[304,768]{1,0:T(8,128)(2,1)} %pad.12.refs_0_, f32[3,768]{1,0:T(4,128)} %refs_1_.10, f32[3,768]{1,0:T(4,128)} %refs_4_.1, s32[8,1]{1,0:T(8,128)} %fusion.4.refs_3_.refs_2_, bf16[304,768]{1,0:T(8,128)(2,1)} %get-tuple-element.70.refs_4_.refs_5_, ...), custom_call_target="tpu_custom_call" | custom-call | flops 4000000000 | bytes 6604832 | tf_op jit(solution)/shard_map/mix_image/pallas_call | solution.py:82
  234.1 1.3 slice.10.refs_2_
  235.4 6.4 %mlp_text.1 = bf16[462,512]{1,0:T(8,128)(2,1)} custom-call(f32[464,512]{1,0:T(8,128)} %get-tuple-element.102.refs_0_, bf16[464,512]{1,0:T(8,128)(2,1)} %get-tuple-element.103.refs_1_, bf16[8,128]{1,0:T(8,128)(2,1)} %slice.10.refs_2_, bf16[1024,512]{1,0:T(8,128)(2,1)} %copy-done.15, bf16[1024,512]{1,0:T(8,128)(2,1)} %bitcast.68, ...), custom_call_target="tpu_custom_call" | custom-call | flops 8000000000 | bytes 5621760 | tf_op jit(solution)/shard_map/mlp_text/pallas_call | solution.py:82
  241.7 8.2 %mlp_image.1 = bf16[300,768]{1,0:T(8,128)(2,1)} custom-call(f32[304,768]{1,0:T(8,128)} %get-tuple-element.73.refs_0_, bf16[304,768]{1,0:T(8,128)(2,1)} %get-tuple-element.74.refs_1_, bf16[8,128]{1,0:T(8,128)(2,1)} %slice.10.refs_2_, bf16[1536,768]{1,0:T(8,128)(2,1)} %copy-done.8, bf16[1536,768]{1,0:T(8,128)(2,1)} %bitcast.13.refs_6_.refs_4_, ...), custom_call_target="tpu_custom_call" | custom-call | flops 8000000000 | bytes 10840064 | tf_op jit(solution)/shard_map/mlp_image/pallas_call | solution.py:82
  250.0 4.2 %last_text.1 = (f32[512,128]{1,0:T(8,128)}, f32[512,128]{1,0:T(8,128)}, f32[512,128]{1,0:T(8,128)}, f32[128,512]{1,0:T(8,128)}, f32[3,512]{1,0:T(4,128)}, /*index=5*/f32[3,512]{1,0:T(4,128)}) custom-call(bf16[256,512]{1,0:T(8,128)(2,1)} %get-tuple-element.104.refs_0_, bf16[512,128]{1,0:T(8,128)(2,1)} %get-tuple-element.122.refs_1_, ...), custom_call_target="tpu_custom_call" | custom-call | flops 1000000000 | bytes 1843200 | tf_op jit(solution)/shard_map/last_text/pallas_call | solution.py:82
  254.1 2.0 maximum_bitcast_fusion.1
  257.2 6.2 %last_image.1 = (f32[192,768]{1,0:T(8,128)}, f32[192,768]{1,0:T(8,128)}, f32[192,768]{1,0:T(8,128)}, f32[192,768]{1,0:T(8,128)}, f32[3,768]{1,0:T(4,128)}, /*index=5*/f32[3,768]{1,0:T(4,128)}) custom-call(bf16[256,768]{1,0:T(8,128)(2,1)} %get-tuple-element.88.refs_0_, bf16[192,768]{1,0:T(8,128)(2,1)} %get-tuple-element.120.refs_1_, ...), custom_call_target="tpu_custom_call" | custom-call | flops 1000000000 | bytes 3747840 | tf_op jit(solution)/shard_map/last_image/pallas_call | solution.py:82
  263.4 2.7 %maximum_bitcast_fusion = f32[768,3,192]{0,2,1:T(8,128)} fusion(f32[1,192,768]{2,1,0:T(8,128)} %bitcast.72, f32[1,192,768]{2,1,0:T(8,128)} %bitcast.71, f32[1,192,768]{2,1,0:T(8,128)} %bitcast.70), kind=kLoop, calls=%fused_computation | loop fusion | flops 884736 | bytes 3538944 | tf_op jit(solution)/shard_map/transpose | solution.py:647
  (83 shorter events, 12.4 us)
Async XLA Ops:
  0.7 14.1 %copy-start.17 = (bf16[512,512]{1,0:T(8,128)(2,1)S(1)}, bf16[512,512]{1,0:T(8,128)(2,1)}, u32[]{:S(2)}) copy-start(bf16[512,512]{1,0:T(8,128)(2,1)} %param.31) | copy-start | bytes 1572868
  1.8 13.0 %copy-start.18 = (bf16[512,512]{1,0:T(8,128)(2,1)S(1)}, bf16[512,512]{1,0:T(8,128)(2,1)}, u32[]{:S(2)}) copy-start(bf16[512,512]{1,0:T(8,128)(2,1)} %param.32) | copy-start | bytes 1572868
  3.5 6.5 %collective-permute-start.3 = (bf16[512,128]{1,0:T(8,128)(2,1)S(1)}, bf16[512,128]{1,0:T(8,128)(2,1)S(1)}, u32[]{:S(2)}, u32[]{:S(2)}) collective-permute-start(bf16[512,128]{1,0:T(8,128)(2,1)S(1)} %get-tuple-element.123), channel_id=1, source_target_pairs={{0,2},{2,0},{1,3},{3,1},{4,6},{6,4},{5,7},{7,5},{8,10},{10,8},{9,1... | collective-permute-start | bytes 393224 | tf_op jit(solution)/shard_map/ppermute | solution.py:552
  10.8 11.2 %all-to-all-start.1 = ((bf16[4,512,128]{2,1,0:T(8,128)(2,1)}), bf16[4,512,128]{2,1,0:T(8,128)(2,1)S(1)}, u32[]{:S(2)}, u32[]{:S(2)}) async-start(bf16[4,512,128]{2,1,0:T(8,128)(2,1)} %broadcast_in_dim.49), calls=%async_computation.1 | async-start | bytes 1048576 | tf_op jit(solution)/shard_map/all_to_all | solution.py:554
  14.8 1.7 copy-start.15
  14.9 12.2 %copy-start.1 = (bf16[768,3,192]{0,2,1:T(8,128)(2,1)S(1)}, bf16[768,3,192]{0,2,1:T(8,128)(2,1)}, u32[]{:S(2)}) copy-start(bf16[768,3,192]{0,2,1:T(8,128)(2,1)} %param.21) | copy-start | bytes 2654212
  14.9 12.2 %copy-start.5 = (bf16[192,768]{1,0:T(8,128)(2,1)S(1)}, bf16[192,768]{1,0:T(8,128)(2,1)}, u32[]{:S(2)}) copy-start(bf16[192,768]{1,0:T(8,128)(2,1)} %refs_2_.9) | copy-start | bytes 884740
  14.9 7.1 %collective-permute-start.10 = (bf16[256,512]{1,0:T(8,128)(2,1)S(1)}, bf16[256,512]{1,0:T(8,128)(2,1)S(1)}, u32[]{:S(2)}, u32[]{:S(2)}) collective-permute-start(bf16[256,512]{1,0:T(8,128)(2,1)S(1)} %dynamic-slice_bitcast_fusion.1), channel_id=1, source_target_pairs={{0,2},{2,0},{1,3},{3,1},{4,6},{6,4},{5,7},{7,5},{8,10},{10,8},{9,1... | collective-permute-start | bytes 786440 | tf_op jit(solution)/shard_map/ppermute | solution.py:552
  22.0 23.4 %copy-start.7 = (bf16[4,512,128]{2,1,0:T(8,128)(2,1)}, bf16[4,512,128]{2,1,0:T(8,128)(2,1)S(1)}, u32[]{:S(2)}) copy-start(bf16[4,512,128]{2,1,0:T(8,128)(2,1)S(1)} %all-to-all-done.1.refs_6_.refs_11_.refs_8_) | copy-start | bytes 1572868
  23.2 15.5 %all-to-all-start.4 = ((bf16[4,256,512]{2,1,0:T(8,128)(2,1)}), bf16[4,256,512]{2,1,0:T(8,128)(2,1)S(1)}, u32[]{:S(2)}, u32[]{:S(2)}) async-start(bf16[4,256,512]{2,1,0:T(8,128)(2,1)} %broadcast_in_dim.52), calls=%async_computation.4 | async-start | bytes 2097152 | tf_op jit(solution)/shard_map/all_to_all | solution.py:554
  27.9 16.7 %copy-start.6 = (bf16[512,3,128]{2,0,1:T(8,128)(2,1)S(1)}, bf16[512,3,128]{2,0,1:T(8,128)(2,1)}, u32[]{:S(2)}) copy-start(bf16[512,3,128]{2,0,1:T(8,128)(2,1)} %param.29) | copy-start | bytes 1179652
  27.9 6.8 %collective-permute-start = (bf16[192,768]{1,0:T(8,128)(2,1)S(1)}, bf16[192,768]{1,0:T(8,128)(2,1)}, u32[]{:S(2)}, u32[]{:S(2)}) collective-permute-start(bf16[192,768]{1,0:T(8,128)(2,1)S(1)} %get-tuple-element.121), channel_id=1, source_target_pairs={{0,2},{2,0},{1,3},{3,1},{4,6},{6,4},{5,7},{7,5},{8,10},{10,8},{9,1... | collective-permute-start | bytes 884744 | tf_op jit(solution)/shard_map/ppermute | solution.py:552
  38.7 2.2 copy-start.13
  40.9 5.0 %copy-start.24 = (s32[24]{0:T(128)S(1)}, s32[24]{0:T(128)}, u32[]{:S(2)}) copy-start(s32[24]{0:T(128)} %param.34) | copy-start | bytes 292
  40.9 18.1 %all-to-all-start = ((bf16[4,192,768]{2,1,0:T(8,128)(2,1)}), bf16[4,192,768]{2,1,0:T(8,128)(2,1)S(1)}, u32[]{:S(2)}, u32[]{:S(2)}) async-start(bf16[4,192,768]{2,1,0:T(8,128)(2,1)} %broadcast_in_dim.25), calls=%async_computation | async-start | bytes 2359296 | tf_op jit(solution)/shard_map/all_to_all | solution.py:554
  45.4 3.1 %collective-permute-start.4 = (bf16[4,512,128]{2,1,0:T(8,128)(2,1)}, bf16[4,512,128]{2,1,0:T(8,128)(2,1)S(1)}, u32[]{:S(2)}, u32[]{:S(2)}) collective-permute-start(bf16[4,512,128]{2,1,0:T(8,128)(2,1)} %pad_maximum_fusion.1.refs_5_.refs_10_.refs_7_), channel_id=1, source_target_pairs={{0,1},{1,0},{2,3},{3,2},{4,5},{5,4},{6,7},{7,6},{8,9},{9,8},{10,11... | collective-permute-start | bytes 1572872 | tf_op jit(solution)/shard_map/ppermute | solution.py:555
  45.5 3.1 %collective-permute-start.5 = (bf16[4,512,128]{2,1,0:T(8,128)(2,1)S(1)}, bf16[4,512,128]{2,1,0:T(8,128)(2,1)}, u32[]{:S(2)}, u32[]{:S(2)}) collective-permute-start(bf16[4,512,128]{2,1,0:T(8,128)(2,1)S(1)} %all-to-all-done.1.refs_6_.refs_11_.refs_8_), channel_id=1, source_target_pairs={{0,1},{1,0},{2,3},{3,2},{4,5},{5,4},{6,7},{7,6},{8,9},{9,8},{10,11... | collective-permute-start | bytes 1572872 | tf_op jit(solution)/shard_map/ppermute | solution.py:555
  48.5 0.8 copy-start.16
  56.2 7.6 %copy-start.9 = (bf16[768,768]{1,0:T(8,128)(2,1)S(1)}, bf16[768,768]{1,0:T(8,128)(2,1)}, u32[]{:S(2)}) copy-start(bf16[768,768]{1,0:T(8,128)(2,1)} %param.23) | copy-start | bytes 3538948
  59.0 35.7 %copy-start.2 = (bf16[4,192,768]{2,1,0:T(8,128)(2,1)}, bf16[4,192,768]{2,1,0:T(8,128)(2,1)S(1)}, u32[]{:S(2)}) copy-start(bf16[4,192,768]{2,1,0:T(8,128)(2,1)S(1)} %all-to-all-done.refs_6_.refs_8_.refs_11_) | copy-start | bytes 3538948
  59.1 29.4 %all-to-all-start.7 = ((bf16[32,24,512]{2,1,0:T(8,128)(2,1)}), bf16[32,24,512]{2,1,0:T(8,128)(2,1)}, u32[]{:S(2)}, u32[]{:S(2)}) async-start(bf16[32,24,512]{2,1,0:T(8,128)(2,1)} %bitcast.69), calls=%async_computation.7 | async-start | bytes 1572864 | tf_op jit(solution)/shard_map/all_to_all | solution.py:590
  63.8 1.3 copy-start.10
  65.2 1.5 copy-start.8
  66.7 21.7 %collective-permute-start.7 = (bf16[384,768]{1,0:T(8,128)(2,1)S(1)}, bf16[384,768]{1,0:T(8,128)(2,1)S(1)}, u32[]{:S(2)}, u32[]{:S(2)}) collective-permute-start(bf16[384,768]{1,0:T(8,128)(2,1)S(1)} %dynamic-slice_bitcast_fusion), channel_id=1, source_target_pairs={{0,2},{2,0},{1,3},{3,1},{4,6},{6,4},{5,7},{7,5},{8,10},{10,8},{9,1... | collective-permute-start | bytes 1769480 | tf_op jit(solution)/shard_map/ppermute | solution.py:552
  90.0 32.8 %all-to-all-start.3 = ((bf16[4,384,768]{2,1,0:T(8,128)(2,1)}), bf16[4,384,768]{2,1,0:T(8,128)(2,1)}, u32[]{:S(2)}, u32[]{:S(2)}) async-start(bf16[4,384,768]{2,1,0:T(8,128)(2,1)} %broadcast_in_dim.51), calls=%async_computation.3 | async-start | bytes 4718592 | tf_op jit(solution)/shard_map/all_to_all | solution.py:554
  94.5 1.2 copy-start.20
  94.6 1.0 copy-start.3
  94.6 2.9 %collective-permute-start.1 = (bf16[4,192,768]{2,1,0:T(8,128)(2,1)S(1)}, bf16[4,192,768]{2,1,0:T(8,128)(2,1)S(1)}, u32[]{:S(2)}, u32[]{:S(2)}) collective-permute-start(bf16[4,192,768]{2,1,0:T(8,128)(2,1)S(1)} %pad_maximum_fusion.refs_5_.refs_7_.refs_10_), channel_id=1, source_target_pairs={{0,1},{1,0},{2,3},{3,2},{4,5},{5,4},{6,7},{7,6},{8,9},{9,8},{10,11... | collective-permute-start | bytes 3538952 | tf_op jit(solution)/shard_map/ppermute | solution.py:555
  94.8 4.4 %collective-permute-start.2 = (bf16[4,192,768]{2,1,0:T(8,128)(2,1)S(1)}, bf16[4,192,768]{2,1,0:T(8,128)(2,1)S(1)}, u32[]{:S(2)}, u32[]{:S(2)}) collective-permute-start(bf16[4,192,768]{2,1,0:T(8,128)(2,1)S(1)} %all-to-all-done.refs_6_.refs_8_.refs_11_), channel_id=1, source_target_pairs={{0,1},{1,0},{2,3},{3,2},{4,5},{5,4},{6,7},{7,6},{8,9},{9,8},{10,11... | collective-permute-start | bytes 3538952 | tf_op jit(solution)/shard_map/ppermute | solution.py:555
  97.0 11.7 %copy-start.22 = (bf16[8,512]{1,0:T(8,128)(2,1)S(1)}, bf16[8,512]{1,0:T(8,128)(2,1)}, u32[]{:S(2)}) copy-start(bf16[8,512]{1,0:T(8,128)(2,1)} %get-tuple-element.76) | copy-start | bytes 24580
  97.5 1.7 copy-start.11
  99.2 1.0 copy-start.12
  123.5 18.7 %copy-start.14 = (bf16[4,256,512]{2,1,0:T(8,128)(2,1)S(1)}, bf16[4,256,512]{2,1,0:T(8,128)(2,1)}, u32[]{:S(2)}) copy-start(bf16[4,256,512]{2,1,0:T(8,128)(2,1)} %copy-done.13) | copy-start | bytes 3145732
  123.5 15.5 %all-to-all-start.2 = ((bf16[16,8,1280]{2,1,0:T(8,128)(2,1)}), bf16[16,8,1280]{2,1,0:T(8,128)(2,1)S(1)}, u32[]{:S(2)}, u32[]{:S(2)}) async-start(bf16[16,8,1280]{2,1,0:T(8,128)(2,1)} %broadcast_in_dim.50), calls=%async_computation.2 | async-start | bytes 655360 | tf_op jit(solution)/shard_map/all_to_all | solution.py:585
  128.3 17.1 %collective-permute-start.8 = (bf16[4,384,768]{2,1,0:T(8,128)(2,1)}, bf16[4,384,768]{2,1,0:T(8,128)(2,1)}, u32[]{:S(2)}, u32[]{:S(2)}) collective-permute-start(bf16[4,384,768]{2,1,0:T(8,128)(2,1)} %bitcast.63), channel_id=1, source_target_pairs={{0,1},{1,0},{2,3},{3,2},{4,5},{5,4},{6,7},{7,6},{8,9},{9,8},{10,11... | collective-permute-start | bytes 7077896 | tf_op jit(solution)/shard_map/ppermute | solution.py:555
  128.4 18.4 %collective-permute-start.9 = (bf16[4,384,768]{2,1,0:T(8,128)(2,1)}, bf16[4,384,768]{2,1,0:T(8,128)(2,1)}, u32[]{:S(2)}, u32[]{:S(2)}) collective-permute-start(bf16[4,384,768]{2,1,0:T(8,128)(2,1)} %all-to-all-done.3), channel_id=1, source_target_pairs={{0,1},{1,0},{2,3},{3,2},{4,5},{5,4},{6,7},{7,6},{8,9},{9,8},{10,11... | collective-permute-start | bytes 7077896 | tf_op jit(solution)/shard_map/ppermute | solution.py:555
  139.0 7.8 %copy-start.21 = (bf16[16,8,1280]{2,1,0:T(8,128)(2,1)}, bf16[16,8,1280]{2,1,0:T(8,128)(2,1)S(1)}, u32[]{:S(2)}) copy-start(bf16[16,8,1280]{2,1,0:T(8,128)(2,1)S(1)} %all-to-all-done.2) | copy-start | bytes 983044
  139.0 47.0 %all-to-all-start.5 = ((bf16[32,32,768]{2,1,0:T(8,128)(2,1)}), bf16[32,32,768]{2,1,0:T(8,128)(2,1)S(1)}, u32[]{:S(2)}, u32[]{:S(2)}) async-start(bf16[32,32,768]{2,1,0:T(8,128)(2,1)} %bitcast.61), calls=%async_computation.5 | async-start | bytes 3145728 | tf_op jit(solution)/shard_map/all_to_all | solution.py:590
  142.0 3.4 %collective-permute-start.11 = (bf16[4,256,512]{2,1,0:T(8,128)(2,1)}, bf16[4,256,512]{2,1,0:T(8,128)(2,1)}, u32[]{:S(2)}, u32[]{:S(2)}) collective-permute-start(bf16[4,256,512]{2,1,0:T(8,128)(2,1)} %bitcast.74), channel_id=1, source_target_pairs={{0,1},{1,0},{2,3},{3,2},{4,5},{5,4},{6,7},{7,6},{8,9},{9,8},{10,11... | collective-permute-start | bytes 3145736 | tf_op jit(solution)/shard_map/ppermute | solution.py:555
  142.2 4.6 %collective-permute-start.12 = (bf16[4,256,512]{2,1,0:T(8,128)(2,1)S(1)}, bf16[4,256,512]{2,1,0:T(8,128)(2,1)}, u32[]{:S(2)}, u32[]{:S(2)}) collective-permute-start(bf16[4,256,512]{2,1,0:T(8,128)(2,1)S(1)} %copy-done.14), channel_id=1, source_target_pairs={{0,1},{1,0},{2,3},{3,2},{4,5},{5,4},{6,7},{7,6},{8,9},{9,8},{10,11... | collective-permute-start | bytes 3145736 | tf_op jit(solution)/shard_map/ppermute | solution.py:555
  142.6 4.2 %collective-permute-start.6 = (bf16[128,1280]{1,0:T(8,128)(2,1)S(1)}, bf16[128,1280]{1,0:T(8,128)(2,1)S(1)}, u32[]{:S(2)}, u32[]{:S(2)}) collective-permute-start(bf16[128,1280]{1,0:T(8,128)(2,1)S(1)} %bitcast.77), channel_id=1, source_target_pairs={{0,1},{1,0},{2,3},{3,2},{4,5},{5,4},{6,7},{7,6},{8,9},{9,8},{10,11... | collective-permute-start | bytes 983048 | tf_op jit(solution)/shard_map/ppermute | solution.py:587
  146.8 0.7 copy-start.23
  186.1 14.5 %copy-start = (bf16[32,32,768]{2,1,0:T(8,128)(2,1)}, bf16[32,32,768]{2,1,0:T(8,128)(2,1)S(1)}, u32[]{:S(2)}) copy-start(bf16[32,32,768]{2,1,0:T(8,128)(2,1)S(1)} %all-to-all-done.5) | copy-start | bytes 4718596
  186.1 21.7 %all-to-all-start.8 = ((bf16[32,16,512]{2,1,0:T(8,128)(2,1)}), bf16[32,16,512]{2,1,0:T(8,128)(2,1)S(1)}, u32[]{:S(2)}, u32[]{:S(2)}) async-start(bf16[32,16,512]{2,1,0:T(8,128)(2,1)} %bitcast.76), calls=%async_computation.8 | async-start | bytes 1048576 | tf_op jit(solution)/shard_map/all_to_all | solution.py:590
  207.8 12.7 %copy-start.19 = (bf16[32,16,512]{2,1,0:T(8,128)(2,1)}, bf16[32,16,512]{2,1,0:T(8,128)(2,1)S(1)}, u32[]{:S(2)}) copy-start(bf16[32,16,512]{2,1,0:T(8,128)(2,1)S(1)} %all-to-all-done.8) | copy-start | bytes 1572868
  207.8 48.4 %all-to-all-start.6 = ((bf16[32,24,768]{2,1,0:T(8,128)(2,1)}), bf16[32,24,768]{2,1,0:T(8,128)(2,1)S(1)}, u32[]{:S(2)}, u32[]{:S(2)}) async-start(bf16[32,24,768]{2,1,0:T(8,128)(2,1)} %bitcast.64), calls=%async_computation.6 | async-start | bytes 2359296 | tf_op jit(solution)/shard_map/all_to_all | solution.py:590
  256.2 1.0 copy-start.4
